TPU v7x, 512 devices: a whole 4x4x16 slice. The times are simulated.
512 devices in a mesh: dp: 64 (over x, z), pipe: 8 (over y, core).
Axes of the slice: x: 4, y: 4, z: 16, core: 2. Of those that a mesh axis runs over, the one named last changes fastest.
Arguments:
- grad_partials: bfloat16 [8, 64, 64, 5376], P('pipe', 'dp'), may hold values from -0.796875 to 0.796875
- master: float32 [64, 5376], P('dp'), may hold values from -0.078125 to 0.078125
- moment_one: float32 [64, 5376], P('dp'), may hold values from -2 to 2
- moment_two: float32 [64, 5376], P('dp'), may hold values from 0.01 to 1
- token_rows: int32 [16384], P('dp'), may hold values from 0 to 63
- input_gain: float32 [5376], replicated, may hold values from 0.1 to 1.9
- key_weight: bfloat16 [5376, 1024], P('dp', 'pipe'), may hold values from -0.078125 to 0.078125
- key_gain: float32 [128], replicated, may hold values from 0.1 to 1.9
Outputs:
- new_master: float32 [64, 5376], P('dp')
- new_moment_one: float32 [64, 5376], P('dp')
- new_moment_two: float32 [64, 5376], P('dp')
- section_input: bfloat16 [8, 16384, 5376], P('pipe', 'dp')
- section_keys: bfloat16 [8, 16384, 1024], P('pipe', 'dp')
All inputs are finite; a program needn't handle non-finite values.
Results may differ from a plain program's by a relative error of at most 0.0065.
Values may be sent and summed in bfloat16 or wider, within the bound.
A program may use at most 128 MiB of HBM per device.

v0:
```python
import jax
import jax.numpy as jnp
from jax import lax
from jax.sharding import PartitionSpec as P

D = 5376
HEAD_DIM = 128


def head_norm(raw_keys, key_gain):
    blocks = raw_keys.reshape(raw_keys.shape[0], -1, HEAD_DIM)
    scaled = (
        blocks * lax.rsqrt(jnp.mean(blocks * blocks, axis=-1, keepdims=True) + 1e-06) * key_gain
    )
    return scaled.reshape(raw_keys.shape).astype(jnp.bfloat16)


def adam_update(gradient, master, moment_one, moment_two):
    new_moment_one = 0.9 * moment_one + 0.1 * gradient
    new_moment_two = 0.95 * moment_two + 0.05 * gradient * gradient
    correct_one = 1.0 - 0.9**10
    correct_two = 1.0 - 0.95**10
    update = new_moment_one / correct_one / (jnp.sqrt(new_moment_two / correct_two) + 1e-08)
    new_master = master - 0.001 * update
    return (new_master, new_moment_one, new_moment_two)


def shards(
    grad_partials, master, moment_one, moment_two, token_rows, input_gain, key_weight, key_gain
):
    section_index = lax.axis_index("pipe")
    pipe_count = lax.axis_size("pipe")
    tied_section = jnp.logical_or(section_index == 0, section_index == pipe_count - 1)
    local_grad = grad_partials[0, 0]
    picked = local_grad.astype(jnp.float32)
    section_part = lax.psum_scatter(
        jnp.where(tied_section, picked, jnp.zeros_like(picked)),
        "dp",
        scatter_dimension=0,
        tiled=True,
    )
    gradient = lax.psum(section_part, "pipe")
    new_master, new_moment_one, new_moment_two = adam_update(
        gradient, master, moment_one, moment_two
    )
    table = lax.all_gather(new_master.astype(jnp.bfloat16), "dp", axis=0, tiled=True)
    window_rows = table.shape[0]
    one_hot = (token_rows[:, None] == jnp.arange(window_rows, dtype=jnp.int32)[None, :]).astype(
        jnp.bfloat16
    )
    looked = jnp.dot(one_hot, table, preferred_element_type=jnp.float32)
    embedded = (looked * jnp.float32(D**0.5)).astype(jnp.bfloat16)
    wide = embedded.astype(jnp.float32)
    normed = (
        wide * lax.rsqrt(jnp.mean(wide * wide, axis=-1, keepdims=True) + 1e-06) * input_gain
    ).astype(jnp.bfloat16)
    weight_cols = lax.all_gather(key_weight, "pipe", axis=1, tiled=True)
    raw_keys = jnp.dot(
        normed,
        lax.all_gather(weight_cols, "dp", axis=0, tiled=True),
        preferred_element_type=jnp.float32,
    )
    keys = head_norm(raw_keys, key_gain)
    receiving = section_index == 1 % pipe_count
    section_input = jnp.where(receiving, embedded, jnp.zeros_like(embedded))[None]
    section_keys = jnp.where(receiving, keys, jnp.zeros_like(keys))[None]
    return (new_master, new_moment_one, new_moment_two, section_input, section_keys)


def solution(mesh):
    in_specs = (
        P("pipe", "dp", None, None),
        P("dp", None),
        P("dp", None),
        P("dp", None),
        P("dp"),
        P(),
        P("dp", "pipe"),
        P(),
    )
    out_specs = (
        P("dp", None),
        P("dp", None),
        P("dp", None),
        P("pipe", "dp", None),
        P("pipe", "dp", None),
    )
    return jax.shard_map(shards, mesh=mesh, in_specs=in_specs, out_specs=out_specs, check_vma=False)
```

profile of v0, /device:TPU:1, one launch (start us, length us, event | category | flops | bytes accessed | tf_op | source)
XLA Modules:
  0.0 485.5 jit_solution(5907264818291309225)
XLA Ops:
  7.2 0.0 copy-start
  7.2 0.0 copy-start.2
  7.2 0.0 copy-start.5
  7.2 0.0 copy-start.4
  7.2 0.0 copy-start.3
  7.2 0.0 all-reduce.3.cloned.1.call-start
  7.3 0.0 copy-start.7
  7.3 2.3 select_bitcast_fusion.1
  9.6 0.0 all-reduce.3.cloned.1.call-update
  9.6 0.0 all-gather.4.cloned.1.call-start
  9.6 0.0 copy-done.2
  9.6 18.9 %all_gather.10 = bf16[84,1024]{1,0:T(8,128)(2,1)} all-gather(bf16[84,128]{1,0:T(8,128)(2,1)S(1)} %copy-done.2), channel_id=1, replica_groups=mesh['dp'=64,'pipe'=8] {'pipe'}, dimensions={1}, use_global_device_ids=true | all-gather | bytes 193536 | tf_op jit(solution)/shard_map/all_gather | solution.py:57
  28.6 0.0 all-gather.4.cloned.1.call-update
  28.6 1.3 dynamic-slice
  29.9 0.0 copy-done
  29.9 254.4 %all-reduce.3.cloned.1.call-done = f32[64,5376]{1,0:T(8,128)} async-done(((f32[64,5376]{1,0:T(8,128)}), f32[64,5376]{1,0:T(8,128)}) %all-reduce.3.cloned.1.call-update) | async-done | bytes 1376272
  284.3 1.6 constant_dynamic-slice_fusion
  285.9 30.2 %psum.7 = f32[1,5376]{1,0:T(1,128)S(1)} all-reduce(f32[1,5376]{1,0:T(1,128)S(1)} %constant_dynamic-slice_fusion), channel_id=1, replica_groups=mesh['dp'=64,'pipe'=8] {'pipe'}, use_global_device_ids=true, to_apply=%region_1.2 | all-reduce | flops 5376 | bytes 43008 | tf_op jit(solution)/shard_map/psum | solution.py:42
  316.1 0.0 copy-done.5
  316.1 0.0 copy-done.4
  316.1 0.0 copy-done.3
  316.1 0.8 convert_bitcast_fusion
  316.9 79.8 %all-gather = bf16[64,1,5376]{2,1,0:T(2,128)(2,1)S(1)} all-gather(bf16[1,1,5376]{2,1,0:T(2,128)(2,1)S(1)} %get-tuple-element.5), channel_id=1, replica_groups=mesh['dp'=64,'pipe'=8] {'dp'}, dimensions={0}, use_global_device_ids=true | all-gather | bytes 698880 | tf_op jit(solution)/shard_map/all_gather | solution.py:46
  396.7 0.0 copy-done.7
  396.7 1.0 fusion.1
  397.7 0.0 copy-start.1
  397.7 1.5 copy-done.1
  399.2 1.7 select_bitcast_fusion
  400.9 0.0 copy-start.6
  400.9 54.8 %all-gather.4.cloned.1.call-done = bf16[64,84,1024]{2,1,0:T(8,128)(2,1)} async-done(((bf16[1,84,1024]{2,1,0:T(8,128)(2,1)}), bf16[64,84,1024]{2,1,0:T(8,128)(2,1)}) %all-gather.4.cloned.1.call-update) | async-done | bytes 11010064 | tf_op jit(solution)/shard_map/all_gather | solution.py:60
  455.7 13.9 %reshape.41 = bf16[5376,1024]{1,0:T(8,128)(2,1)} reshape(bf16[64,84,1024]{2,1,0:T(8,128)(2,1)} %all-gather.4.cloned.1.call-done) | data formatting | bytes 22020096
  469.6 0.0 copy-done.6
  469.6 6.7 %fusion.4 = f32[256,1024]{1,0:T(8,128)S(1)} fusion(bf16[5376,1024]{1,0:T(8,128)(2,1)} %reshape.41, bf16[256,5376]{1,0:T(8,128)(2,1)} %copy-done.1, f32[5376]{0:T(1024)S(1)} %copy-done.6, f32[256]{0:T(256)S(1)} %add_rsqrt_fusion.1), kind=kOutput, calls=%fused_computation.7 | convolution fusion | flops 2824077312 | bytes 14833664 | tf_op jit(solution)/shard_map/dot_general | solution.py:58
  476.3 0.1 multiply_bitcast_fusion
  476.4 0.2 copy.17
  476.6 0.3 reduce_sum.19
  477.0 0.1 copy.14
  477.1 0.1 copy.15
  477.2 0.3 mul.108
  477.5 1.1 fusion.13
  (3 shorter events, 0.0 us)
Async XLA Ops:
  7.2 22.7 %copy-start = (f32[128]{0:T(128)S(1)}, f32[128]{0:T(128)}, u32[]{:S(2)}) copy-start(f32[128]{0:T(128)} %param.15) | copy-start | bytes 1540
  7.2 2.5 copy-start.2
  7.2 308.9 %copy-start.5 = (f32[1,5376]{1,0:T(1,128)S(1)}, f32[1,5376]{1,0:T(1,128)}, u32[]{:S(2)}) copy-start(f32[1,5376]{1,0:T(1,128)} %param.11) | copy-start | bytes 64516
  7.2 308.9 %copy-start.4 = (f32[1,5376]{1,0:T(1,128)S(1)}, f32[1,5376]{1,0:T(1,128)}, u32[]{:S(2)}) copy-start(f32[1,5376]{1,0:T(1,128)} %param.10) | copy-start | bytes 64516
  7.2 308.9 %copy-start.3 = (f32[1,5376]{1,0:T(1,128)S(1)}, f32[1,5376]{1,0:T(1,128)}, u32[]{:S(2)}) copy-start(f32[1,5376]{1,0:T(1,128)} %param.9) | copy-start | bytes 64516
  7.2 277.1 %all-reduce.3.cloned.1.call-start = ((), (), s32[]{:S(2)}) async-start(), calls=%async_computation.1 | async-start | bytes 2752512
  7.3 389.4 %copy-start.7 = (s32[256]{0:T(256)S(1)}, s32[256]{0:T(256)}, u32[]{:S(2)}) copy-start(s32[256]{0:T(256)} %param.12) | copy-start | bytes 3076
  9.6 446.1 %all-gather.4.cloned.1.call-start = ((), (), s32[]{:S(2)}) async-start(), calls=%async_computation | async-start | bytes 11714560 | tf_op jit(solution)/shard_map/all_gather | solution.py:60
  397.7 1.5 copy-start.1
  400.9 68.7 %copy-start.6 = (f32[5376]{0:T(1024)S(1)}, f32[5376]{0:T(1024)}, u32[]{:S(2)}) copy-start(f32[5376]{0:T(1024)} %param.13) | copy-start | bytes 64516
Sparse Core Ops, SparseCore 0:
  12.1 272.1 all-reduce.2
  287.2 168.4 all-gather.3
where the time goes:
time: 489 us; the launch traced here: 485 us
  waiting for transfers between devices  309 us (63%)
  blocking collectives  129 us (26%)
  local copies, waits for them, and re-layouts  19.1 us (4%)
  between operations  14.2 us (3%)
  matrix products  7.71 us (2%)
  other arithmetic  6.3 us (1%)
    unnamed x3, waiting for transfers between devices  254 us
    all_gather x1, blocking collectives, shards(): lax.all_gather(new_master.astype(jnp.bfloat16), 'dp', axis=0, tiled=True)  79.8 us
    all_gather x1, waiting for transfers between devices, shards(): lax.all_gather(weight_cols, 'dp', axis=0, tiled=True)  54.8 us
    psum x1, blocking collectives, shards(): gradient = lax.psum(section_part, 'pipe')  30.2 us
    all_gather x1, blocking collectives, shards(): weight_cols = lax.all_gather(key_weight, 'pipe', axis=1, tiled=True)  18.9 us
    unnamed x20, local copies, waits for them, and re-layouts  18.6 us
  transfers between devices with their start and end apart: 2, of which 2 were waited for; matrix products, arithmetic and copies ran while one was open for 1% of the time, Pallas kernels for 0%

commit v1 on v0

v1 whole, which is shorter than its diff:
```python
import jax
import jax.numpy as jnp
from jax import lax
from jax.experimental import pallas as pl
from jax.experimental.pallas import tpu as pltpu
from jax.sharding import PartitionSpec as P

MESH = pl.DeviceIdType.MESH
HEAD_DIM = 128
LANES = 128
NX, NZ, NP = 4, 16, 8
D = 5376
NCH = D // LANES
PAD = 48
WROWS = 84
WPAD = 96
KC = 11
KW = KC * LANES
HEADS2 = 2 * HEAD_DIM

(
    XS, XR, XL, ZS, ZR, YS, YR0, YR1, W0S, W0R, WAS, WAR, WBS, WB1, WB2, WB3,
    ES, ER, KS, KR, FS, FR, PS, PR, OUT,
) = range(25)


def first_chunk(x):
    return (x // 2) * 21 + lax.rem(x, 2) * 10


def comm_kernel(
    grad, master, moment_one, moment_two, weight, gain,
    table_out, keys_out, master_out, one_out, two_out,
    gx, zs, zb, zr, yr, prior, erow, ezr, ef, block, full, part, wc, wp, wz, wf, wk, kp, sem,
):
    dp = lax.axis_index("dp")
    pipe = lax.axis_index("pipe")
    x, z = dp // NZ, lax.rem(dp, NZ)
    y, core = pipe // 2, lax.rem(pipe, 2)
    holder = jnp.logical_or(pipe == 0, pipe == NP - 1)
    ringer = jnp.logical_or(holder, core == 1)
    last = pipe == NP - 1
    lead = pipe == 1
    odd = core == 1

    def at(x_to, z_to, pipe_to):
        return (x_to * NZ + z_to, pipe_to)

    def send(src, dst, sent, arrived, where):
        pltpu.make_async_remote_copy(
            src_ref=src, dst_ref=dst, send_sem=sem.at[sent], recv_sem=sem.at[arrived],
            device_id=where, device_id_type=MESH,
        ).start()

    def wait_for(like, which):
        pltpu.make_async_copy(like, like, sem.at[which]).wait()

    barrier = pltpu.get_barrier_semaphore()

    def tell(where):
        pl.semaphore_signal(barrier, inc=1, device_id=where, device_id_type=MESH)

    @pl.when(ringer)
    def _():
        @pl.loop(1, NZ)
        def _(k):
            tell(at(x, lax.rem(z + k, NZ), pipe))

        for k in range(1, NX):
            tell(at(lax.rem(x + k, NX), z, pipe))

    @pl.when(pipe != 0)
    def _():
        tell((dp, 0))

    @pl.when(jnp.logical_not(last))
    def _():
        tell((dp, NP - 1))

    @pl.when(jnp.logical_and(odd, jnp.logical_not(lead)))
    def _():
        tell((dp, pipe - 1))

    @pl.when(lead)
    def _():
        for k in range(NX):
            for q in range(3, NP, 2):
                if k > 0 or q < NP - 1:
                    tell(at(lax.rem(x + k, NX), z, q))

    wc[...] = jnp.zeros_like(wc)
    wc[0:WROWS, :] = weight[...]

    peers = NZ - 1 + NX - 1
    for q in range(NP):
        count = (peers if q in (0, NP - 1) or q % 2 else 0) + (NP - 1 if q in (0, NP - 1) else 0)
        count += 1 if q % 2 == 0 and q != 0 else 0
        count += NX if q % 2 and q not in (1, NP - 1) else 0
        count += NX - 1 if q == NP - 1 else 0

        @pl.when(pipe == q)
        def _(count=count):
            pl.semaphore_wait(barrier, count)

    @pl.when(holder)
    def _():
        for k in range(1, NX):
            to = lax.rem(x + k, NX)
            rows = pl.ds(pl.multiple_of(to * NZ, NZ), NZ)
            send(grad.at[0, 0, rows, :], gx.at[x], XS, XR, at(to, z, pipe))
        rows = pl.ds(pl.multiple_of(x * NZ, NZ), NZ)
        pltpu.make_async_copy(grad.at[0, 0, rows, :], gx.at[x], sem.at[XL]).start()

    @pl.when(jnp.logical_not(odd))
    def _():
        send(wc, wp.at[:, 0:LANES], W0S, W0R, (dp, pipe + 1))

    mine = lax.rem(z, 4)

    @pl.when(odd)
    def _():
        wp[:, LANES:HEADS2] = wc[...]
        wait_for(wc, W0R)
        for k in range(1, 4):
            send(wp, wz.at[mine, z // 4], WAS, WAR, at(x, lax.rem(z + 4 * k, NZ), pipe))
        wz[mine, z // 4] = wp[...]

    def weights_on():
        wait_for(wz.at[0, 0:3], WAR)
        send(wz.at[mine], wz.at[mine], WBS, WB1, at(x, lax.rem(z + 1, NZ), pipe))
        send(wz.at[mine], wz.at[mine], WBS, WB2, at(x, lax.rem(z + NZ - 1, NZ), pipe))
        two = z + 2 + lax.rem(z, 2) * (NZ - 4)
        send(wz.at[mine], wz.at[mine], WBS, WB3, at(x, lax.rem(two, NZ), pipe))

    @pl.when(jnp.logical_and(odd, jnp.logical_not(last)))
    def _():
        weights_on()

    prior[...] = jnp.zeros_like(prior)

    @pl.loop(0, NCH)
    def _(j):
        lanes = pl.ds(pl.multiple_of(j * LANES, LANES), LANES)
        prior[0, pl.ds(j, 1), :] = master[:, lanes]
        prior[1, pl.ds(j, 1), :] = moment_one[:, lanes]
        prior[2, pl.ds(j, 1), :] = moment_two[:, lanes]

    @pl.when(holder)
    def _():
        zs[...] = jnp.zeros_like(zs)
        wait_for(gx.at[0], XL)
        wait_for(gx.at[0:3], XR)

        @pl.loop(0, NCH)
        def _(j):
            lanes = pl.ds(pl.multiple_of(j * LANES, LANES), LANES)
            total = gx[0, :, lanes].astype(jnp.float32)
            for k in range(1, NX):
                total = total + gx[k, :, lanes].astype(jnp.float32)
            zs[pl.ds(j, NZ, stride=PAD), :] = total

        zb[...] = zs[...].reshape(NZ, PAD, LANES).astype(jnp.bfloat16)

        @pl.loop(1, NZ)
        def _(k):
            to = lax.rem(z + k, NZ)
            send(zb.at[to], zr.at[z], ZS, ZR, at(x, to, pipe))

        zr[z] = zb[z]

    @pl.when(last)
    def _():
        weights_on()

    @pl.when(holder)
    def _():
        wait_for(zr.at[0 : NZ - 1], ZR)
        total = zr[0].astype(jnp.float32)
        for k in range(1, NZ):
            total = total + zr[k].astype(jnp.float32)

        @pl.when(pipe == 0)
        def _():
            yr[0] = total
            for q in range(1, NP):
                send(yr.at[0], yr.at[0], YS, YR0, (dp, q))

        @pl.when(last)
        def _():
            yr[1] = total
            for q in range(NP - 1):
                send(yr.at[1], yr.at[1], YS, YR1, (dp, q))

    @pl.when(pipe != 0)
    def _():
        wait_for(yr.at[0], YR0)

    @pl.when(jnp.logical_not(last))
    def _():
        wait_for(yr.at[1], YR1)

    gradient = yr[0] + yr[1]
    new_one = 0.9 * prior[1] + 0.1 * gradient
    new_two = 0.95 * prior[2] + 0.05 * gradient * gradient
    correct_one = 1.0 - 0.9**10
    correct_two = 1.0 - 0.95**10
    update = new_one / correct_one / (jnp.sqrt(new_two / correct_two) + 1e-08)
    new_master = prior[0] - 0.001 * update

    @pl.when(odd)
    def _():
        table = new_master.astype(jnp.bfloat16).astype(jnp.float32)
        erow[...] = (table * jnp.float32(D**0.5)).astype(jnp.bfloat16)

        @pl.loop(1, NZ)
        def _(k):
            send(erow, ezr.at[z], ES, ER, at(x, lax.rem(z + k, NZ), pipe))

        ezr[z] = erow[...]

    master_out[...] = new_master
    one_out[...] = new_one
    two_out[...] = new_two

    @pl.when(odd)
    def _():
        wait_for(wz.at[0], WB1)
        wait_for(wz.at[0], WB2)
        wait_for(wz.at[0], WB3)
        side = lax.rem(x, 2)
        spare = pl.multiple_of((1 - side) * NZ * WROWS, 64)
        wk[pl.ds(spare, 64), :] = jnp.zeros((64, HEADS2), jnp.bfloat16)

        @pl.loop(0, 4)
        def _(g):
            for k in range(4):
                wf[WROWS * k : WROWS * (k + 1), :] = wz[k, g, 0:WROWS, :].astype(jnp.float32)
            start = pl.multiple_of(side * 64 + g * 4 * WROWS, 16)
            wk[pl.ds(start, 4 * WROWS), :] = wf[...].astype(jnp.bfloat16)

        wait_for(ezr.at[0 : NZ - 1], ER)
        ef[...] = ezr[...].astype(jnp.float32).reshape(NZ * PAD, LANES)

        @pl.loop(0, NCH)
        def _(j):
            lanes = pl.ds(pl.multiple_of(j * LANES, LANES), LANES)
            block[:, lanes] = ef[pl.ds(j, NZ, stride=PAD), :].astype(jnp.bfloat16)

        def features(x_of):
            return pl.ds(pl.multiple_of(first_chunk(x_of) * LANES, LANES), KW)

        for k in range(1, NX):
            to = lax.rem(x + k, NX)
            send(block.at[:, features(to)], part.at[x], KS, KR, at(to, z, pipe))

        @pl.when(lead)
        def _():
            for k in range(1, NX):
                send(block, full.at[x], FS, FR, at(lax.rem(x + k, NX), z, pipe))
            full[x] = block[...]

        part[x] = block[:, features(x)]
        wait_for(part.at[0:3], KR)
        scaled = part[...].reshape(NX * NZ, KW).astype(jnp.float32) * gain[:, features(x)]
        product = jnp.dot(
            scaled.astype(jnp.bfloat16), wk[...], preferred_element_type=jnp.float32
        )
        slot = y * NX + x
        kp[slot] = product.astype(jnp.bfloat16)
        for k in range(NX):
            to = lax.rem(x + k, NX)

            def share(to=to):
                send(kp.at[slot], kp.at[slot], PS, PR, at(to, z, 1))

            if k:
                share()
            else:
                pl.when(jnp.logical_not(lead))(share)

    @pl.when(lead)
    def _():
        wait_for(full.at[0:3], FR)
        out = pltpu.make_async_copy(full, table_out, sem.at[OUT])
        out.start()
        squares = jnp.zeros((NX * NZ, LANES), jnp.float32)
        for j in range(NCH):
            wide = full[:, :, LANES * j : LANES * (j + 1)].astype(jnp.float32)
            wide = wide.reshape(NX * NZ, LANES)
            squares = squares + wide * wide
        scale = lax.rsqrt(jnp.sum(squares, axis=-1, keepdims=True) / D + 1e-06)
        wait_for(kp.at[0 : NX * NP // 2 - 1], PR)
        for s in range(NP // 2):
            raw = kp[s * NX].astype(jnp.float32)
            for k in range(1, NX):
                raw = raw + kp[s * NX + k].astype(jnp.float32)
            raw = raw * scale
            for h in range(2):
                head = raw[:, h * HEAD_DIM : (h + 1) * HEAD_DIM]
                keys_out[:, s * HEADS2 + h * HEAD_DIM : s * HEADS2 + (h + 1) * HEAD_DIM] = (
                    head * lax.rsqrt(jnp.mean(head * head, axis=-1, keepdims=True) + 1e-06)
                )
        out.wait()

    @pl.when(holder)
    def _():
        wait_for(gx.at[0:3], XS)
        wait_for(zr.at[0 : NZ - 1], ZS)
        for q in range(NP - 1):
            wait_for(yr.at[0], YS)

    @pl.when(jnp.logical_not(odd))
    def _():
        wait_for(wc, W0S)

    @pl.when(odd)
    def _():
        wait_for(wz.at[0, 0:3], WAS)
        wait_for(wz.at[0:3], WBS)
        wait_for(ezr.at[0 : NZ - 1], ES)
        wait_for(part.at[0:3], KS)
        wait_for(kp.at[0:3], PS)

        @pl.when(lead)
        def _():
            wait_for(full.at[0:3], FS)

        @pl.when(jnp.logical_not(lead))
        def _():
            wait_for(kp.at[0], PS)


TOKEN_BLOCK = 64


def lookup_kernel(
    table, keys, key_gain, tokens, master, one, two,
    master_out, one_out, two_out, section_input, section_keys,
):
    lead = lax.axis_index("pipe") == 1

    @pl.when(pl.program_id(0) == 0)
    def _():
        @pl.loop(0, NCH)
        def _(j):
            lanes = pl.ds(pl.multiple_of(j * LANES, LANES), LANES)
            master_out[:, lanes] = master[pl.ds(j, 1), :]
            one_out[:, lanes] = one[pl.ds(j, 1), :]
            two_out[:, lanes] = two[pl.ds(j, 1), :]

    @pl.when(lead)
    def _():
        rows = table.shape[0]
        count = section_input.shape[1]
        start = pl.multiple_of(pl.program_id(0) * count, count)
        hot = lax.broadcasted_iota(jnp.int32, (count, rows), 1) == tokens[pl.ds(start, count), :]
        hot = hot.astype(jnp.bfloat16)
        section_input[0] = jnp.dot(
            hot, table[...], preferred_element_type=jnp.float32
        ).astype(jnp.bfloat16)
        gains = jnp.concatenate([key_gain[...]] * (keys.shape[1] // HEAD_DIM), axis=1)
        rounded = (keys[...] * gains).astype(jnp.bfloat16)
        section_keys[0] = jnp.dot(
            hot, rounded, preferred_element_type=jnp.float32
        ).astype(jnp.bfloat16)

    @pl.when(jnp.logical_not(lead))
    def _():
        section_input[...] = jnp.zeros_like(section_input)
        section_keys[...] = jnp.zeros_like(section_keys)


def shards(
    grad_partials, master, moment_one, moment_two, token_rows, input_gain, key_weight, key_gain
):
    rows, kvw = NX * NZ, NP * HEAD_DIM
    bf16, f32 = jnp.bfloat16, jnp.float32
    vmem = pl.BlockSpec(memory_space=pltpu.VMEM)
    hbm = pl.BlockSpec(memory_space=pl.ANY)
    line = jax.ShapeDtypeStruct((PAD, LANES), f32)
    table, keys, row, row_one, row_two = pl.pallas_call(
        comm_kernel,
        out_shape=(
            jax.ShapeDtypeStruct((NX, NZ, D), bf16),
            jax.ShapeDtypeStruct((rows, kvw), f32),
            line, line, line,
        ),
        in_specs=[hbm, vmem, vmem, vmem, vmem, vmem],
        out_specs=(hbm, vmem, vmem, vmem, vmem),
        scratch_shapes=[
            pltpu.VMEM((NX, NZ, D), bf16),
            pltpu.VMEM((NZ * PAD, LANES), f32),
            pltpu.VMEM((NZ, PAD, LANES), bf16),
            pltpu.VMEM((NZ, PAD, LANES), bf16),
            pltpu.VMEM((2, PAD, LANES), f32),
            pltpu.VMEM((3, PAD, LANES), f32),
            pltpu.VMEM((PAD, LANES), bf16),
            pltpu.VMEM((NZ, PAD, LANES), bf16),
            pltpu.VMEM((NZ * PAD, LANES), f32),
            pltpu.VMEM((NZ, D), bf16),
            pltpu.VMEM((NX, NZ, D), bf16),
            pltpu.VMEM((NX, NZ, KW), bf16),
            pltpu.VMEM((WPAD, LANES), bf16),
            pltpu.VMEM((WPAD, HEADS2), bf16),
            pltpu.VMEM((4, 4, WPAD, HEADS2), bf16),
            pltpu.VMEM((4 * WROWS, HEADS2), f32),
            pltpu.VMEM((KW, HEADS2), bf16),
            pltpu.VMEM((NX * NP // 2, rows, HEADS2), bf16),
            pltpu.SemaphoreType.DMA((25,)),
        ],
        compiler_params=pltpu.CompilerParams(
            collective_id=0, has_side_effects=True, vmem_limit_bytes=32 * 2**20
        ),
        name="sum_step_gather",
    )(grad_partials, master, moment_one, moment_two, key_weight, input_gain.reshape(1, D))

    count = token_rows.shape[0]
    whole = pl.BlockSpec((1, D), lambda i: (0, 0))
    new_master, new_one, new_two, section_input, section_keys = pl.pallas_call(
        lookup_kernel,
        grid=(count // TOKEN_BLOCK,),
        out_shape=(
            jax.ShapeDtypeStruct((1, D), f32),
            jax.ShapeDtypeStruct((1, D), f32),
            jax.ShapeDtypeStruct((1, D), f32),
            jax.ShapeDtypeStruct((1, count, D), bf16),
            jax.ShapeDtypeStruct((1, count, kvw), bf16),
        ),
        in_specs=[vmem] * 7,
        out_specs=(
            whole, whole, whole,
            pl.BlockSpec((1, TOKEN_BLOCK, D), lambda i: (0, i, 0)),
            pl.BlockSpec((1, TOKEN_BLOCK, kvw), lambda i: (0, i, 0)),
        ),
        compiler_params=pltpu.CompilerParams(vmem_limit_bytes=32 * 2**20),
        name="look_up",
    )(
        table.reshape(rows, D), keys, key_gain.reshape(1, HEAD_DIM), token_rows.reshape(count, 1),
        row, row_one, row_two,
    )
    return new_master, new_one, new_two, section_input, section_keys


def solution(mesh):
    in_specs = (
        P("pipe", "dp", None, None),
        P("dp", None),
        P("dp", None),
        P("dp", None),
        P("dp"),
        P(),
        P("dp", "pipe"),
        P(),
    )
    out_specs = (
        P("dp", None),
        P("dp", None),
        P("dp", None),
        P("pipe", "dp", None),
        P("pipe", "dp", None),
    )
    return jax.shard_map(shards, mesh=mesh, in_specs=in_specs, out_specs=out_specs, check_vma=False)
```

time: 489 us -> 70.7 us (0.14)
  waiting for transfers between devices: 309 us -> 0 us
  blocking collectives: 129 us -> 0 us
  Pallas kernels: 0 us -> 63.3 us
  between operations: 14.2 us -> 0.67 us
  local copies, waits for them, and re-layouts: 19.1 us -> 6.23 us
  matrix products: 7.71 us -> 0 us
  other arithmetic: 6.3 us -> 0 us
    unnamed x3 -> x0, waiting for transfers between devices: 254 us -> none
    all_gather x2 -> x0, blocking collectives: 98.7 us -> none  [the longest x1 79.8 us: shards(): lax.all_gather(new_master.astype(jnp.bfloat16), 'dp', axis=0, tiled=True)]
    pallas_call x0 -> x2, Pallas kernels: none -> 63.3 us  [the longest x1 59.9 us: shards(): pl.pallas_call(comm_kernel, out_shape=(jax.ShapeDtypeStruct((NX, NZ, D),...]
    all_gather x1 -> x0, waiting for transfers between devices: 54.8 us -> none  [shards(): lax.all_gather(weight_cols, 'dp', axis=0, tiled=True)]
    psum x1 -> x0, blocking collectives: 30.2 us -> none  [shards(): gradient = lax.psum(section_part, 'pipe')]
    unnamed x20 -> x12, local copies, waits for them, and re-layouts: 18.6 us -> 4.67 us
    dot_general x2 -> x0, matrix products: 7.71 us -> none  [the longest x1 6.7 us: shards(): jnp.dot(normed, lax.all_gather(weight_cols, 'dp', axis=0, tiled=True), pr...]
  transfers between devices with their start and end apart: 2 -> 0, of which waited for: 2 -> 0; matrix products, arithmetic and copies ran while one was open for 1% -> 0% of each run, Pallas kernels for 0% -> 0%
where the time goes in v1:
time: 70.7 us; the launch traced here: 70.2 us
  Pallas kernels  63.3 us (90%)
  local copies, waits for them, and re-layouts  6.23 us (9%)
    pallas_call x1, Pallas kernels, shards(): pl.pallas_call(comm_kernel, out_shape=(jax.ShapeDtypeStruct((NX, NZ, D),...  59.9 us
    unnamed x12, local copies, waits for them, and re-layouts  4.67 us
    pallas_call x1, Pallas kernels, shards(): pl.pallas_call(lookup_kernel, grid=(count // TOKEN_BLOCK,), out_shape=(ja...  3.39 us

profile of v1, /device:TPU:1, one launch (start us, length us, event | category | flops | bytes accessed | tf_op | source)
XLA Modules:
  0.0 70.2 jit_solution(6734370093935417237)
XLA Ops:
  0.6 0.8 %reshape.22.gain = f32[1,5376]{1,0:T(1,128)S(1)} reshape(f32[5376]{0:T(1024)} %param.13) | data formatting | bytes 43008 | tf_op jit(solution)/shard_map/reshape | solution.py:415
  1.4 0.8 %copy.13.tokens = s32[256,1]{1,0:T(8,128)S(1)} copy(s32[256,1]{0,1:T(1,128)} %bitcast.5) | data formatting | bytes 2048 | tf_op jit(solution)/shard_map/reshape | solution.py:438
  2.2 0.0 copy-start
  2.2 1.1 %copy-done = bf16[1,1,64,5376]{3,2,1,0:T(8,128)(2,1)S(1)} copy-done((bf16[1,1,64,5376]{3,2,1,0:T(8,128)(2,1)S(1)}, bf16[1,1,64,5376]{3,2,1,0:T(8,128)(2,1)}, u32[]{:S(2)}) %copy-start) | copy-done | bytes 688152
  3.3 0.0 copy-start.1
  3.3 0.7 %copy-done.1 = bf16[84,128]{1,0:T(8,128)(2,1)S(1)} copy-done((bf16[84,128]{1,0:T(8,128)(2,1)S(1)}, bf16[84,128]{1,0:T(8,128)(2,1)}, u32[]{:S(2)}) %copy-start.1) | copy-done | bytes 21528
  4.0 0.0 copy-start.2
  4.0 0.7 %copy-done.2 = f32[1,5376]{1,0:T(1,128)S(1)} copy-done((f32[1,5376]{1,0:T(1,128)S(1)}, f32[1,5376]{1,0:T(1,128)}, u32[]{:S(2)}) %copy-start.2) | copy-done | bytes 21528
  4.8 0.0 copy-start.3
  4.8 0.7 %copy-done.3 = f32[1,5376]{1,0:T(1,128)S(1)} copy-done((f32[1,5376]{1,0:T(1,128)S(1)}, f32[1,5376]{1,0:T(1,128)}, u32[]{:S(2)}) %copy-start.3) | copy-done | bytes 21528
  5.5 0.0 copy-start.4
  5.5 0.7 %copy-done.4 = f32[1,5376]{1,0:T(1,128)S(1)} copy-done((f32[1,5376]{1,0:T(1,128)S(1)}, f32[1,5376]{1,0:T(1,128)}, u32[]{:S(2)}) %copy-start.4) | copy-done | bytes 21528
  6.2 59.9 %sum_step_gather.1 = (bf16[4,16,5376]{2,1,0:T(8,128)(2,1)S(1)}, f32[64,1024]{1,0:T(8,128)S(1)}, f32[48,128]{1,0:T(8,128)S(1)}, f32[48,128]{1,0:T(8,128)S(1)}, f32[48,128]{1,0:T(8,128)S(1)}) custom-call(bf16[1,1,64,5376]{3,2,1,0:T(8,128)(2,1)S(1)} %copy-done, f32[1,5376]{1,0:T(1,128)S(1)} %copy-done.2, f32[1,5376]{1,0:T(1,128)S(1)} %copy-done.3, ...), custom_call_target="tpu_custom_call" | custom-call | tf_op jit(solution)/shard_map/sum_step_gather/pallas_call | solution.py:381
  66.1 0.0 copy-start.5
  66.1 0.6 copy-done.5
  66.8 3.4 %look_up.1 = (f32[1,5376]{1,0:T(1,128)}, f32[1,5376]{1,0:T(1,128)}, f32[1,5376]{1,0:T(1,128)}, bf16[1,256,5376]{2,1,0:T(8,128)(2,1)}, bf16[1,256,1024]{2,1,0:T(8,128)(2,1)}) custom-call(bf16[64,5376]{1,0:T(8,128)(2,1)S(1)} %bitcast.3, f32[64,1024]{1,0:T(8,128)S(1)} %get-tuple-element.11.keys, f32[1,128]{1,0:T(1,128)S(1)} %bitcast.4, ...), custom_call_target="tpu_custom_call" | custom-call | tf_op jit(solution)/shard_map/look_up/pallas_call | solution.py:419
Async XLA Ops:
  2.2 1.1 %copy-start = (bf16[1,1,64,5376]{3,2,1,0:T(8,128)(2,1)S(1)}, bf16[1,1,64,5376]{3,2,1,0:T(8,128)(2,1)}, u32[]{:S(2)}) copy-start(bf16[1,1,64,5376]{3,2,1,0:T(8,128)(2,1)} %grad.1) | copy-start | bytes 2064388
  3.3 0.7 %copy-start.1 = (bf16[84,128]{1,0:T(8,128)(2,1)S(1)}, bf16[84,128]{1,0:T(8,128)(2,1)}, u32[]{:S(2)}) copy-start(bf16[84,128]{1,0:T(8,128)(2,1)} %weight.1) | copy-start | bytes 64516
  4.0 0.7 %copy-start.2 = (f32[1,5376]{1,0:T(1,128)S(1)}, f32[1,5376]{1,0:T(1,128)}, u32[]{:S(2)}) copy-start(f32[1,5376]{1,0:T(1,128)} %master.1) | copy-start | bytes 64516
  4.8 0.7 %copy-start.3 = (f32[1,5376]{1,0:T(1,128)S(1)}, f32[1,5376]{1,0:T(1,128)}, u32[]{:S(2)}) copy-start(f32[1,5376]{1,0:T(1,128)} %moment_one.1) | copy-start | bytes 64516
  5.5 0.7 %copy-start.4 = (f32[1,5376]{1,0:T(1,128)S(1)}, f32[1,5376]{1,0:T(1,128)}, u32[]{:S(2)}) copy-start(f32[1,5376]{1,0:T(1,128)} %moment_two.1) | copy-start | bytes 64516
  66.1 0.7 copy-start.5

commit v2 on v1

v2 whole, which is shorter than its diff:
```python
import jax
import jax.numpy as jnp
from jax import lax
from jax.experimental import pallas as pl
from jax.experimental.pallas import tpu as pltpu
from jax.sharding import PartitionSpec as P

MESH = pl.DeviceIdType.MESH
HEAD_DIM = 128
LANES = 128
NX, NZ, NP = 4, 16, 8
D = 5376
NCH = D // LANES
PAD = 48
WROWS = 84
WPAD = 96
KC = 11
KW = KC * LANES
HEADS2 = 2 * HEAD_DIM
VMEM_BYTES = 60 * 2**20

(
    XS, XR, ZS, ZR, RP, RM, YS, YR0, YR1, W0S, W0R, WAS, WM, WP, W8, WBS, WB0, WB1, WB2, WB3,
    ES, EM, EP, ER, KS, KR, FS, FR, PS, PR, LM, L1, L2, LW, LG, LK, O1, O2, O3,
) = range(39)
REACH = 4


def first_chunk(x):
    return (x // 2) * 21 + lax.rem(x, 2) * 10


def comm_kernel(
    grad, master, moment_one, moment_two, weight, gain, key_gain,
    table_out, keys_out, step_out,
    gx, zs, zb, zr, zp, zm, zq, yr, state, prior, erow, ezr, ef, block, full, part, wv, wc, wp, wg, wz, wf, wk, kp,
    gv, gl, kg, step, keys, sem,
):
    dp = lax.axis_index("dp")
    pipe = lax.axis_index("pipe")
    x, z = dp // NZ, lax.rem(dp, NZ)
    y = pipe // 2
    far = y == NP // 2 - 1
    worker = jnp.where(far, 2 * y, 2 * y + 1) == pipe
    mate = jnp.where(lax.rem(pipe, 2) == 0, pipe + 1, pipe - 1)
    source = jnp.logical_or(pipe == 0, pipe == NP - 1)
    lead, last = pipe == 1, pipe == NP - 2
    reducer = jnp.logical_or(lead, last)

    def at(x_to, z_to, pipe_to):
        return (x_to * NZ + z_to, pipe_to)

    def send(src, dst, sent, arrived, where):
        pltpu.make_async_remote_copy(
            src_ref=src, dst_ref=dst, send_sem=sem.at[sent], recv_sem=sem.at[arrived],
            device_id=where, device_id_type=MESH,
        ).start()

    def wait_for(like, which):
        pltpu.make_async_copy(like, like, sem.at[which]).wait()

    barrier = pltpu.get_barrier_semaphore()

    def tell(where):
        pl.semaphore_signal(barrier, inc=1, device_id=where, device_id_type=MESH)

    def away(k):
        return lax.rem(z + k + NZ, NZ)

    near = [k for k in range(-REACH, REACH + 1) if k]

    two = 2 - 4 * lax.rem(z, 2)

    @pl.when(worker)
    def _():
        for k in near:
            tell(at(x, away(k), pipe))
        for k in range(1, NX):
            tell(at(lax.rem(x + k, NX), z, pipe))
        for k in (0, 1, -1, -two):
            tell(at(x, away(k), mate))

    @pl.when(reducer)
    def _():
        for k in range(1, NX):
            tell(at(lax.rem(x + k, NX), z, mate))

    @pl.when(jnp.logical_not(worker))
    def _():
        tell(at(x, away(REACH), pipe))
        tell(at(x, away(-REACH), pipe))

    @pl.when(jnp.logical_or(pipe == 2, pipe == 4))
    def _():
        tell((dp, mate))

    @pl.when(jnp.logical_not(lead))
    def _():
        tell((dp, 1))

    @pl.when(jnp.logical_not(last))
    def _():
        tell((dp, NP - 2))

    @pl.when(lead)
    def _():
        for k in range(NX):
            for q in (3, 5, 6):
                if k > 0 or q != 6:
                    tell(at(lax.rem(x + k, NX), z, q))

    def load(src, dst, which):
        copy = pltpu.make_async_copy(src, dst, sem.at[which])
        copy.start()
        return copy

    load_weight = load(weight, wv, LW)
    load_state = [
        load(master, state.at[0], LM), load(moment_one, state.at[1], L1),
        load(moment_two, state.at[2], L2),
    ]
    load_gain = load(gain, gv, LG)
    load_key_gain = load(key_gain, kg, LK)

    peers = len(near) + NX - 1
    counts = {
        0: 6 + NX - 1, NP - 1: 6 + NX - 1, 2: 6, 4: 6,
        1: peers + NP - 1, 6: peers + NP - 1 + NX - 1, 3: peers + NX + 1, 5: peers + NX + 1,
    }
    for q, count in counts.items():

        @pl.when(pipe == q)
        def _(count=count):
            pl.semaphore_wait(barrier, count)

    @pl.when(source)
    def _():
        for k in range(NX):
            to = lax.rem(x + k, NX)
            rows = pl.ds(pl.multiple_of(to * NZ, NZ), NZ)
            send(grad.at[0, 0, rows, :], gx.at[x], XS, XR, at(to, z, mate))

    load_weight.wait()
    wc[...] = jnp.zeros_like(wc)
    wide = wv[...].astype(jnp.float32)
    for q in range(4):
        @pl.when(lax.rem(z, 4) == q)
        def _(q=q):
            wf[...] = jnp.zeros_like(wf)
            wf[4 * q : 4 * q + WROWS, :] = wide
            wc[...] = wf[...].astype(jnp.bfloat16)

    for high in (False, True):
        lanes = slice(LANES, HEADS2) if high else slice(0, LANES)

        @pl.when((lax.rem(pipe, 2) == 1) == high)
        def _(lanes=lanes):
            @pl.when(worker)
            def _():
                send(wc, wp.at[:, lanes], W0S, W0R, (dp, mate))

            @pl.when(jnp.logical_not(worker))
            def _():
                wp[:, lanes] = wc[...]

    @pl.when(jnp.logical_not(worker))
    def _():
        mine = lax.rem(z, 4)
        wait_for(wc, W0R)
        send(wp, wg.at[z // 4], WAS, WM, at(x, away(REACH), pipe))
        send(wp, wg.at[z // 4], WAS, WP, at(x, away(-REACH), pipe))
        wg[z // 4] = wp[...]
        wait_for(wp, WM)
        back = lax.rem(z // 4 + 3, 4)
        send(wg.at[back], wg.at[back], WAS, W8, at(x, away(REACH), pipe))
        wait_for(wp, WP)
        wait_for(wp, W8)
        for k, which in ((two, WB3), (1, WB1), (-1, WB2), (0, WB0)):
            send(wg, wz.at[mine], WBS, which, at(x, away(k), mate))

    prior[...] = jnp.zeros_like(prior)
    for copy in load_state:
        copy.wait()
    for j in range(NCH):
        lanes = slice(j * LANES, (j + 1) * LANES)
        prior[0, j : j + 1, :] = state[0, :, lanes]
        prior[1, j : j + 1, :] = state[1, :, lanes]
        prior[2, j : j + 1, :] = state[2, :, lanes]

    load_gain.wait()
    load_key_gain.wait()

    def weights_join():
        wait_for(wz.at[0], WB0)
        wait_for(wz.at[0], WB1)
        wait_for(wz.at[0], WB2)
        wait_for(wz.at[0], WB3)
        side = lax.rem(x, 2)
        spare = pl.multiple_of((1 - side) * NZ * WROWS, 64)
        wk[pl.ds(spare, 64), :] = jnp.zeros((64, HEADS2), jnp.bfloat16)
        for g in range(4):
            start = pl.multiple_of(side * 64 + g * 4 * WROWS, 16)

            def put(row, value):
                wk[pl.ds(pl.multiple_of(start + row, 16), value.shape[0]), :] = value

            for k in range(4):
                edge = wz[k, g, 0:16, :]
                if k:
                    edge = edge + wz[k - 1, g, 80:96, :]
                put(80 * k, edge)
                put(80 * k + 16, wz[k, g, 16:80, :])
            put(320, wz[3, g, 80:96, :])
        for j in range(NCH):
            gl[:, j * LANES : (j + 1) * LANES] = gv[j : j + 1, :]

    def row_sum(refs):
        total = refs[0].astype(jnp.float32)
        for ref in refs[1:]:
            total = total + ref.astype(jnp.float32)
        return total

    @pl.when(reducer)
    def _():
        zs[...] = jnp.zeros_like(zs)
        wait_for(gx, XR)
        for j in range(NCH):
            lanes = slice(j * LANES, (j + 1) * LANES)
            total = row_sum([gx[k, :, lanes] for k in range(NX)])
            zs[pl.ds(j, NZ, stride=PAD), :] = total
        zb[...] = zs[...].reshape(NZ, PAD, LANES).astype(jnp.bfloat16)

        for k in range(REACH, 0, -1):
            send(zb.at[away(k + REACH)], zp.at[k - 1], ZS, RP, at(x, away(k), pipe))
            if k < REACH:
                send(zb.at[away(-k - REACH)], zm.at[k - 1], ZS, RM, at(x, away(-k), pipe))
        for k in range(1, REACH):
            send(zb.at[away(k)], zr.at[REACH - k], ZS, ZR, at(x, away(k), pipe))
            send(zb.at[away(-k)], zr.at[REACH + k - 1], ZS, ZR, at(x, away(-k), pipe))

        def pass_up():
            wait_for(zp, RP)
            own = zs[pl.ds(pl.multiple_of(away(REACH) * PAD, PAD), PAD), :]
            zq[0] = (own + row_sum([zp[k] for k in range(REACH)])).astype(jnp.bfloat16)
            send(zq.at[0], zr.at[0], ZS, ZR, at(x, away(REACH), pipe))

        def pass_down():
            wait_for(zm, RM)
            own = zs[pl.ds(pl.multiple_of(away(-REACH) * PAD, PAD), PAD), :]
            zq[1] = (own + row_sum([zm[k] for k in range(REACH - 1)])).astype(jnp.bfloat16)
            send(zq.at[1], zr.at[2 * REACH - 1], ZS, ZR, at(x, away(-REACH), pipe))

        @pl.when(z < NZ // 2)
        def _():
            pass_up()
            pass_down()

        @pl.when(z >= NZ // 2)
        def _():
            pass_down()
            pass_up()

    @pl.when(reducer)
    def _():
        wait_for(zr, ZR)
        own = zs[pl.ds(pl.multiple_of(z * PAD, PAD), PAD), :]
        total = own + row_sum([zr[k] for k in range(2 * REACH)])

        @pl.when(lead)
        def _():
            yr[0] = total
            for q in (3, 5, 6, 0, 2, 4, 7):
                send(yr.at[0], yr.at[0], YS, YR0, (dp, q))

        @pl.when(last)
        def _():
            yr[1] = total
            for q in (1, 3, 5, 0, 2, 4, 7):
                send(yr.at[1], yr.at[1], YS, YR1, (dp, q))

    @pl.when(jnp.logical_not(lead))
    def _():
        wait_for(yr.at[0], YR0)

    @pl.when(jnp.logical_not(last))
    def _():
        wait_for(yr.at[1], YR1)

    gradient = yr[0] + yr[1]
    new_one = 0.9 * prior[1] + 0.1 * gradient
    new_two = 0.95 * prior[2] + 0.05 * gradient * gradient
    correct_one = 1.0 - 0.9**10
    correct_two = 1.0 - 0.95**10
    update = new_one / correct_one / (jnp.sqrt(new_two / correct_two) + 1e-08)
    new_master = prior[0] - 0.001 * update
    step[0] = new_master
    step[1] = new_one
    step[2] = new_two
    keep = pltpu.make_async_copy(step, step_out, sem.at[O1])

    @pl.when(worker)
    def _():
        table = new_master.astype(jnp.bfloat16).astype(jnp.float32)
        erow[...] = (table * jnp.float32(D**0.5)).astype(jnp.bfloat16)
        for k in (4, -4, 3, -3, 2, -2, 1, -1):
            arrives = {REACH: EM, -REACH: EP}.get(k, ER)
            send(erow, ezr.at[z], ES, arrives, at(x, away(k), pipe))
        ezr[z] = erow[...]

    keep.start()

    @pl.when(worker)
    def _():
        def pass_up():
            wait_for(erow, EM)
            row = away(-REACH)
            for k in range(REACH, 0, -1):
                send(ezr.at[row], ezr.at[row], ES, ER, at(x, away(k), pipe))

        def pass_down():
            wait_for(erow, EP)
            row = away(REACH)
            for k in range(REACH - 1, 0, -1):
                send(ezr.at[row], ezr.at[row], ES, ER, at(x, away(-k), pipe))

        @pl.when(z < NZ // 2)
        def _():
            pass_down()
            pass_up()

        @pl.when(z >= NZ // 2)
        def _():
            pass_up()
            pass_down()

        weights_join()

        wait_for(ezr.at[0 : NZ - 3], ER)
        ef[...] = ezr[...].astype(jnp.float32).reshape(NZ * PAD, LANES)

        for j in range(NCH):
            lanes = slice(j * LANES, (j + 1) * LANES)
            block[:, lanes] = ef[pl.ds(j, NZ, stride=PAD), :].astype(jnp.bfloat16)

        def features(x_of):
            return pl.ds(pl.multiple_of(first_chunk(x_of) * LANES, LANES), KW)

        for k in range(1, NX):
            to = lax.rem(x + k, NX)
            send(block.at[:, features(to)], part.at[x], KS, KR, at(to, z, pipe))

        @pl.when(lead)
        def _():
            for k in range(1, NX):
                send(block, full.at[x], FS, FR, at(lax.rem(x + k, NX), z, pipe))
            full[x] = block[...]

        part[x] = block[:, features(x)]
        wait_for(part.at[0:3], KR)
        scaled = part[...].reshape(NX * NZ, KW).astype(jnp.float32) * gl[:, features(x)]
        product = jnp.dot(
            scaled.astype(jnp.bfloat16), wk[...], preferred_element_type=jnp.float32
        )
        slot = y * NX + x
        kp[slot] = product.astype(jnp.bfloat16)
        for k in range(NX):
            to = lax.rem(x + k, NX)

            def share(to=to):
                send(kp.at[slot], kp.at[slot], PS, PR, at(to, z, 1))

            if k:
                share()
            else:
                pl.when(jnp.logical_not(lead))(share)

    @pl.when(lead)
    def _():
        wait_for(full.at[0:3], FR)
        out = pltpu.make_async_copy(full, table_out, sem.at[O2])
        out.start()
        squares = jnp.zeros((NX * NZ, LANES), jnp.float32)
        for j in range(NCH):
            wide = full[:, :, LANES * j : LANES * (j + 1)].astype(jnp.float32)
            wide = wide.reshape(NX * NZ, LANES)
            squares = squares + wide * wide
        scale = lax.rsqrt(jnp.sum(squares, axis=-1, keepdims=True) / D + 1e-06)
        wait_for(kp.at[0 : NX * NP // 2 - 1], PR)
        for s in range(NP // 2):
            raw = kp[s * NX].astype(jnp.float32)
            for k in range(1, NX):
                raw = raw + kp[s * NX + k].astype(jnp.float32)
            raw = raw * scale
            for h in range(2):
                head = raw[:, h * HEAD_DIM : (h + 1) * HEAD_DIM]
                mean = jnp.mean(head * head, axis=-1, keepdims=True)
                first = s * HEADS2 + h * HEAD_DIM
                keys[:, first : first + HEAD_DIM] = (
                    head * lax.rsqrt(mean + 1e-06) * kg[...]
                ).astype(jnp.bfloat16)
        last_out = pltpu.make_async_copy(keys, keys_out, sem.at[O3])
        last_out.start()
        out.wait()
        last_out.wait()

    keep.wait()

    @pl.when(source)
    def _():
        wait_for(gx, XS)

    @pl.when(reducer)
    def _():
        wait_for(ezr.at[0 : NZ - 1], ZS)
        for q in range(NP - 1):
            wait_for(yr.at[0], YS)

    @pl.when(jnp.logical_not(worker))
    def _():
        wait_for(wg.at[0:3], WAS)
        wait_for(wz, WBS)

    @pl.when(worker)
    def _():
        wait_for(wc, W0S)
        wait_for(ezr.at[0 : NZ - 1], ES)
        wait_for(part.at[0:3], KS)
        wait_for(kp.at[0:3], PS)

        @pl.when(lead)
        def _():
            wait_for(full.at[0:3], FS)

        @pl.when(jnp.logical_not(lead))
        def _():
            wait_for(kp.at[0], PS)


PARTS = 6


def look_up_kernel(
    table, keys, step, tokens,
    master_out, one_out, two_out, section_input, section_keys,
    table_v, keys_v, step_v, tokens_v, rows_v, looked, looked_keys, sem,
):
    lead = lax.axis_index("pipe") == 1
    width = D // PARTS

    def move(src, dst, which):
        copy = pltpu.make_async_copy(src, dst, sem.at[which])
        copy.start()
        return copy

    def give(part):
        lanes = slice(part * width, (part + 1) * width)
        return move(looked.at[:, lanes], section_input.at[:, lanes], part)

    load_step = move(step, step_v, 6)

    @pl.when(lead)
    def _():
        load_tokens = move(tokens, tokens_v, 7)
        load_table = move(table, table_v, 8)
        load_keys = move(keys, keys_v, 9)
        load_tokens.wait()
        rows = lax.broadcasted_iota(jnp.int32, (NX * NZ, tokens_v.shape[1]), 0)
        hot = jnp.where(rows == tokens_v[...], 1.0, 0.0).T.astype(jnp.bfloat16)
        load_table.wait()
        gives = []
        for part in range(PARTS):
            lanes = slice(part * width, (part + 1) * width)
            columns = table_v[:, :, lanes].reshape(NX * NZ, width)
            looked[:, lanes] = jnp.dot(
                hot, columns, preferred_element_type=jnp.float32
            ).astype(jnp.bfloat16)
            gives.append(give(part))
        load_keys.wait()
        looked_keys[...] = jnp.dot(
            hot, keys_v[...], preferred_element_type=jnp.float32
        ).astype(jnp.bfloat16)
        gives.append(move(looked_keys, section_keys, 10))
        for copy in gives:
            copy.wait()

    @pl.when(jnp.logical_not(lead))
    def _():
        looked[...] = jnp.zeros_like(looked)
        looked_keys[...] = jnp.zeros_like(looked_keys)
        gives = [give(part) for part in range(PARTS)]
        gives.append(move(looked_keys, section_keys, 10))
        for copy in gives:
            copy.wait()

    load_step.wait()
    for j in range(NCH):
        lanes = slice(j * LANES, (j + 1) * LANES)
        for k in range(3):
            rows_v[k, :, lanes] = step_v[k, j : j + 1, :]
    outs = [
        move(rows_v.at[k], out, 11 + k) for k, out in enumerate((master_out, one_out, two_out))
    ]
    for copy in outs:
        copy.wait()


def shards(
    grad_partials, master, moment_one, moment_two, token_rows, input_gain, key_weight, key_gain
):
    rows, kvw, count = NX * NZ, NP * HEAD_DIM, token_rows.shape[0]
    bf16, f32 = jnp.bfloat16, jnp.float32
    hbm = pl.BlockSpec(memory_space=pl.ANY)
    table, keys, step = pl.pallas_call(
        comm_kernel,
        out_shape=(
            jax.ShapeDtypeStruct((NX, NZ, D), bf16),
            jax.ShapeDtypeStruct((rows, kvw), bf16),
            jax.ShapeDtypeStruct((3, PAD, LANES), f32),
        ),
        in_specs=[hbm] * 7,
        out_specs=(hbm,) * 3,
        scratch_shapes=[
            pltpu.VMEM((NX, NZ, D), bf16),
            pltpu.VMEM((NZ * PAD, LANES), f32),
            pltpu.VMEM((NZ, PAD, LANES), bf16),
            pltpu.VMEM((2 * REACH, PAD, LANES), bf16),
            pltpu.VMEM((REACH, PAD, LANES), bf16),
            pltpu.VMEM((REACH - 1, PAD, LANES), bf16),
            pltpu.VMEM((2, PAD, LANES), bf16),
            pltpu.VMEM((2, PAD, LANES), f32),
            pltpu.VMEM((3, 1, D), f32),
            pltpu.VMEM((3, PAD, LANES), f32),
            pltpu.VMEM((PAD, LANES), bf16),
            pltpu.VMEM((NZ, PAD, LANES), bf16),
            pltpu.VMEM((NZ * PAD, LANES), f32),
            pltpu.VMEM((NZ, D), bf16),
            pltpu.VMEM((NX, NZ, D), bf16),
            pltpu.VMEM((NX, NZ, KW), bf16),
            pltpu.VMEM((WROWS, LANES), bf16),
            pltpu.VMEM((WPAD, LANES), bf16),
            pltpu.VMEM((WPAD, HEADS2), bf16),
            pltpu.VMEM((4, WPAD, HEADS2), bf16),
            pltpu.VMEM((4, 4, WPAD, HEADS2), bf16),
            pltpu.VMEM((WPAD, LANES), f32),
            pltpu.VMEM((KW, HEADS2), bf16),
            pltpu.VMEM((NX * NP // 2, rows, HEADS2), bf16),
            pltpu.VMEM((NCH, LANES), f32),
            pltpu.VMEM((1, D), f32),
            pltpu.VMEM((1, HEAD_DIM), f32),
            pltpu.VMEM((3, PAD, LANES), f32),
            pltpu.VMEM((rows, kvw), bf16),
            pltpu.SemaphoreType.DMA((39,)),
        ],
        compiler_params=pltpu.CompilerParams(
            collective_id=0, has_side_effects=True, vmem_limit_bytes=VMEM_BYTES
        ),
        name="sum_step_gather",
    )(
        grad_partials, master, moment_one, moment_two, key_weight,
        input_gain.reshape(NCH, LANES), key_gain.reshape(1, HEAD_DIM),
    )
    line = jax.ShapeDtypeStruct((1, D), f32)
    new_master, new_one, new_two, section_input, section_keys = pl.pallas_call(
        look_up_kernel,
        out_shape=(
            line, line, line,
            jax.ShapeDtypeStruct((count, D), bf16),
            jax.ShapeDtypeStruct((count, kvw), bf16),
        ),
        in_specs=[hbm] * 4,
        out_specs=(hbm,) * 5,
        scratch_shapes=[
            pltpu.VMEM((NX, NZ, D), bf16),
            pltpu.VMEM((rows, kvw), bf16),
            pltpu.VMEM((3, PAD, LANES), f32),
            pltpu.VMEM((1, count), jnp.int32),
            pltpu.VMEM((3, 1, D), f32),
            pltpu.VMEM((count, D), bf16),
            pltpu.VMEM((count, kvw), bf16),
            pltpu.SemaphoreType.DMA((14,)),
        ],
        compiler_params=pltpu.CompilerParams(vmem_limit_bytes=VMEM_BYTES),
        name="look_up",
    )(table, keys, step, token_rows.reshape(1, count))
    return new_master, new_one, new_two, section_input[None], section_keys[None]


def solution(mesh):
    in_specs = (
        P("pipe", "dp", None, None),
        P("dp", None),
        P("dp", None),
        P("dp", None),
        P("dp"),
        P(),
        P("dp", "pipe"),
        P(),
    )
    out_specs = (
        P("dp", None),
        P("dp", None),
        P("dp", None),
        P("pipe", "dp", None),
        P("pipe", "dp", None),
    )
    return jax.shard_map(shards, mesh=mesh, in_specs=in_specs, out_specs=out_specs, check_vma=False)
```

time: 70.7 us -> 58.6 us (0.83)
  local copies, waits for them, and re-layouts: 6.23 us -> 0 us
  Pallas kernels: 63.3 us -> 57.8 us
    pallas_call x1, Pallas kernels: 59.9 us -> 53.9 us  [shards(): pl.pallas_call(comm_kernel, out_shape=(jax.ShapeDtypeStruct((NX, NZ, D),...]
    unnamed x12 -> x0, local copies, waits for them, and re-layouts: 4.67 us -> none
    reshape x2 -> x0, local copies, waits for them, and re-layouts: 1.56 us -> none  [the longest x1 0.81 us: shards(): token_rows.reshape(count, 1)]
where the time goes in v2:
time: 58.6 us; the launch traced here: 58.4 us
  Pallas kernels  57.8 us (99%)
  between operations  0.64 us (1%)
    pallas_call x1, Pallas kernels, shards(): pl.pallas_call(comm_kernel, out_shape=(jax.ShapeDtypeStruct((NX, NZ, D),...  53.9 us
    pallas_call x1, Pallas kernels, shards(): pl.pallas_call(look_up_kernel, out_shape=(line, line, line, jax.ShapeDtyp...  3.91 us

profile of v2, /device:TPU:1, one launch (start us, length us, event | category | flops | bytes accessed | tf_op | source)
XLA Modules:
  0.0 58.4 jit_solution(12566386788503820385)
XLA Ops:
  0.6 53.9 %sum_step_gather.1 = (bf16[4,16,5376]{2,1,0:T(8,128)(2,1)}, bf16[64,1024]{1,0:T(8,128)(2,1)}, f32[3,48,128]{2,1,0:T(8,128)}) custom-call(bf16[1,1,64,5376]{3,2,1,0:T(8,128)(2,1)} %grad.1, f32[1,5376]{1,0:T(1,128)} %master.1, f32[1,5376]{1,0:T(1,128)} %moment_one.1, f32[1,5376]{1,0:T(1,128)} %moment_two.1, bf16[84,128]{1,0:T(8,128)(2,1)} %weight.1, ...), custom_call_target="tpu_custom_call" | custom-call | tf_op jit(solution)/shard_map/sum_step_gather/pallas_call | solution.py:513
  54.5 3.9 %look_up.1 = (f32[1,5376]{1,0:T(1,128)}, f32[1,5376]{1,0:T(1,128)}, f32[1,5376]{1,0:T(1,128)}, bf16[256,5376]{1,0:T(8,128)(2,1)}, bf16[256,1024]{1,0:T(8,128)(2,1)}) custom-call(bf16[4,16,5376]{2,1,0:T(8,128)(2,1)} %get-tuple-element.13.table, bf16[64,1024]{1,0:T(8,128)(2,1)} %get-tuple-element.14.keys, f32[3,48,128]{2,1,0:T(8,128)} %get-tuple-element.15.step, ...), custom_call_target="tpu_custom_call" | custom-call | tf_op jit(solution)/shard_map/look_up/pallas_call | solution.py:563

commit v3 on v2

--- a/solution.py
+++ b/solution.py
@@ -18,12 +18,20 @@
 KW = KC * LANES
 HEADS2 = 2 * HEAD_DIM
 VMEM_BYTES = 60 * 2**20
+SHARES = {1: slice(0, 2688), 3: slice(2688, 4096), 6: slice(4096, D)}
 
 (
-    XS, XR, ZS, ZR, RP, RM, YS, YR0, YR1, W0S, W0R, WAS, WM, WP, W8, WBS, WB0, WB1, WB2, WB3,
-    ES, EM, EP, ER, KS, KR, FS, FR, PS, PR, LM, L1, L2, LW, LG, LK, O1, O2, O3,
-) = range(39)
+    XS, ZS, YS, YR0, YR1, W0S, W0R, WAS, WB,
+    ES, EM, EP, ER, KS, KR, FS, FR, PS, PR, LM, L1, L2, LW, LG, LK, O1, O2, O3, XR,
+) = range(29)
+THIRDS, BAND = 3, 14
+ZR, RP, RM, WR = XR + THIRDS, XR + 2 * THIRDS, XR + 3 * THIRDS, XR + 4 * THIRDS
+SEMS = WR + NZ
 REACH = 4
+
+
+def place(j):
+    return j // BAND * 16 + j % BAND
 
 
 def first_chunk(x):
@@ -33,7 +41,7 @@
 def comm_kernel(
     grad, master, moment_one, moment_two, weight, gain, key_gain,
     table_out, keys_out, step_out,
-    gx, zs, zb, zr, zp, zm, zq, yr, state, prior, erow, ezr, ef, block, full, part, wv, wc, wp, wg, wz, wf, wk, kp,
+    gx, zs, zb, zr, zp, zm, zq, yr, state, prior, erow, ezr, ef, block, full, part, wv, wc, wp, hz, wz, wf, wk, kp,
     gv, gl, kg, step, keys, sem,
 ):
     dp = lax.axis_index("dp")
@@ -69,16 +77,13 @@
 
     near = [k for k in range(-REACH, REACH + 1) if k]
 
-    two = 2 - 4 * lax.rem(z, 2)
-
     @pl.when(worker)
     def _():
         for k in near:
             tell(at(x, away(k), pipe))
         for k in range(1, NX):
             tell(at(lax.rem(x + k, NX), z, pipe))
-        for k in (0, 1, -1, -two):
-            tell(at(x, away(k), mate))
+        tell((dp, mate))
 
     @pl.when(reducer)
     def _():
@@ -87,8 +92,8 @@
 
     @pl.when(jnp.logical_not(worker))
     def _():
-        tell(at(x, away(REACH), pipe))
-        tell(at(x, away(-REACH), pipe))
+        tell(at(x, away(1), pipe))
+        tell(at(x, away(-1), pipe))
 
     @pl.when(jnp.logical_or(pipe == 2, pipe == 4))
     def _():
@@ -124,7 +129,7 @@
 
     peers = len(near) + NX - 1
     counts = {
-        0: 6 + NX - 1, NP - 1: 6 + NX - 1, 2: 6, 4: 6,
+        0: 3 + NX - 1, NP - 1: 3 + NX - 1, 2: 3, 4: 3,
         1: peers + NP - 1, 6: peers + NP - 1 + NX - 1, 3: peers + NX + 1, 5: peers + NX + 1,
     }
     for q, count in counts.items():
@@ -135,10 +140,15 @@
 
     @pl.when(source)
     def _():
-        for k in range(NX):
-            to = lax.rem(x + k, NX)
-            rows = pl.ds(pl.multiple_of(to * NZ, NZ), NZ)
-            send(grad.at[0, 0, rows, :], gx.at[x], XS, XR, at(to, z, mate))
+        for band in range(THIRDS):
+            lanes = slice(band * BAND * LANES, (band + 1) * BAND * LANES)
+            for k in (2, 1, 3, 0):
+                to = lax.rem(x + k, NX)
+                rows = pl.ds(pl.multiple_of(to * NZ, NZ), NZ)
+                send(
+                    grad.at[0, 0, rows, lanes], gx.at[x, :, lanes], XS, XR + band,
+                    at(to, z, mate),
+                )
 
     load_weight.wait()
     wc[...] = jnp.zeros_like(wc)
@@ -163,38 +173,39 @@
             def _():
                 wp[:, lanes] = wc[...]
 
+    def weights_round(step, away_step, count):
+        row = away(step)
+        if abs(step) < count:
+            send(hz.at[row], hz.at[row], WAS, WR + away_step, at(x, away(-1 if step > 0 else 1), pipe))
+        send(hz.at[row], wz.at[lax.rem(row, 4), row // 4], WAS, WB, (dp, mate))
+
     @pl.when(jnp.logical_not(worker))
     def _():
-        mine = lax.rem(z, 4)
         wait_for(wc, W0R)
-        send(wp, wg.at[z // 4], WAS, WM, at(x, away(REACH), pipe))
-        send(wp, wg.at[z // 4], WAS, WP, at(x, away(-REACH), pipe))
-        wg[z // 4] = wp[...]
-        wait_for(wp, WM)
-        back = lax.rem(z // 4 + 3, 4)
-        send(wg.at[back], wg.at[back], WAS, W8, at(x, away(REACH), pipe))
-        wait_for(wp, WP)
-        wait_for(wp, W8)
-        for k, which in ((two, WB3), (1, WB1), (-1, WB2), (0, WB0)):
-            send(wg, wz.at[mine], WBS, which, at(x, away(k), mate))
+        hz[z] = wp[...]
+        send(hz.at[z], hz.at[z], WAS, WR, at(x, away(1), pipe))
+        send(hz.at[z], hz.at[z], WAS, WR + 8, at(x, away(-1), pipe))
+        send(hz.at[z], wz.at[lax.rem(z, 4), z // 4], WAS, WB, (dp, mate))
+        for step in range(1, 9):
+            wait_for(wp, WR + step - 1)
+            weights_round(-step, step, 8)
+            if step < 8:
+                wait_for(wp, WR + 8 + step - 1)
+                weights_round(step, 8 + step, 7)
 
     prior[...] = jnp.zeros_like(prior)
     for copy in load_state:
         copy.wait()
     for j in range(NCH):
         lanes = slice(j * LANES, (j + 1) * LANES)
-        prior[0, j : j + 1, :] = state[0, :, lanes]
-        prior[1, j : j + 1, :] = state[1, :, lanes]
-        prior[2, j : j + 1, :] = state[2, :, lanes]
+        for k in range(3):
+            prior[k, place(j) : place(j) + 1, :] = state[k, :, lanes]
 
     load_gain.wait()
     load_key_gain.wait()
 
     def weights_join():
-        wait_for(wz.at[0], WB0)
-        wait_for(wz.at[0], WB1)
-        wait_for(wz.at[0], WB2)
-        wait_for(wz.at[0], WB3)
+        wait_for(wz, WB)
         side = lax.rem(x, 2)
         spare = pl.multiple_of((1 - side) * NZ * WROWS, 64)
         wk[pl.ds(spare, 64), :] = jnp.zeros((64, HEADS2), jnp.bfloat16)
@@ -223,46 +234,51 @@
     @pl.when(reducer)
     def _():
         zs[...] = jnp.zeros_like(zs)
-        wait_for(gx, XR)
-        for j in range(NCH):
-            lanes = slice(j * LANES, (j + 1) * LANES)
-            total = row_sum([gx[k, :, lanes] for k in range(NX)])
-            zs[pl.ds(j, NZ, stride=PAD), :] = total
-        zb[...] = zs[...].reshape(NZ, PAD, LANES).astype(jnp.bfloat16)
-
-        for k in range(REACH, 0, -1):
-            send(zb.at[away(k + REACH)], zp.at[k - 1], ZS, RP, at(x, away(k), pipe))
-            if k < REACH:
-                send(zb.at[away(-k - REACH)], zm.at[k - 1], ZS, RM, at(x, away(-k), pipe))
-        for k in range(1, REACH):
-            send(zb.at[away(k)], zr.at[REACH - k], ZS, ZR, at(x, away(k), pipe))
-            send(zb.at[away(-k)], zr.at[REACH + k - 1], ZS, ZR, at(x, away(-k), pipe))
-
-        def pass_up():
-            wait_for(zp, RP)
-            own = zs[pl.ds(pl.multiple_of(away(REACH) * PAD, PAD), PAD), :]
-            zq[0] = (own + row_sum([zp[k] for k in range(REACH)])).astype(jnp.bfloat16)
-            send(zq.at[0], zr.at[0], ZS, ZR, at(x, away(REACH), pipe))
-
-        def pass_down():
-            wait_for(zm, RM)
-            own = zs[pl.ds(pl.multiple_of(away(-REACH) * PAD, PAD), PAD), :]
-            zq[1] = (own + row_sum([zm[k] for k in range(REACH - 1)])).astype(jnp.bfloat16)
-            send(zq.at[1], zr.at[2 * REACH - 1], ZS, ZR, at(x, away(-REACH), pipe))
-
-        @pl.when(z < NZ // 2)
-        def _():
-            pass_up()
-            pass_down()
-
-        @pl.when(z >= NZ // 2)
-        def _():
-            pass_down()
-            pass_up()
-
-    @pl.when(reducer)
-    def _():
-        wait_for(zr, ZR)
+        for band in range(THIRDS):
+            wait_for(gx.at[:, :, 0 : BAND * LANES], XR + band)
+            for j in range(band * BAND, (band + 1) * BAND):
+                lanes = slice(j * LANES, (j + 1) * LANES)
+                total = row_sum([gx[k, :, lanes] for k in range(NX)])
+                zs[pl.ds(place(j), NZ, stride=PAD), :] = total
+            part_rows = slice(16 * band, 16 * (band + 1))
+            for k in range(NZ):
+                zb[k, part_rows, :] = zs[
+                    PAD * k + 16 * band : PAD * k + 16 * (band + 1), :
+                ].astype(jnp.bfloat16)
+
+            def give(row, dst, arrived, k, part_rows=part_rows, band=band):
+                send(
+                    zb.at[row, part_rows], dst.at[part_rows], ZS, arrived + band,
+                    at(x, away(k), pipe),
+                )
+
+            for k in range(REACH, 0, -1):
+                give(away(k + REACH), zp.at[k - 1], RP, k)
+                if k < REACH:
+                    give(away(-k - REACH), zm.at[k - 1], RM, -k)
+            for k in range(1, REACH):
+                give(away(k), zr.at[REACH - k], ZR, k)
+                give(away(-k), zr.at[REACH + k - 1], ZR, -k)
+
+        for band in range(THIRDS):
+            part_rows = slice(16 * band, 16 * (band + 1))
+            ways = (
+                (zp, RP, REACH, 0, 0),
+                (zm, RM, REACH - 1, 1, 2 * REACH - 1),
+            )
+            for ref, arrived, count, slot, there in ways:
+                k = REACH if slot == 0 else -REACH
+                wait_for(ref.at[0:count, part_rows], arrived + band)
+                own = zs[pl.ds(pl.multiple_of(away(k) * PAD + 16 * band, 16), 16), :]
+                passed = own + row_sum([ref[q, part_rows, :] for q in range(count)])
+                zq[slot, part_rows, :] = passed.astype(jnp.bfloat16)
+                send(
+                    zq.at[slot, part_rows], zr.at[there, part_rows], ZS, ZR + band,
+                    at(x, away(k), pipe),
+                )
+
+        for band in range(THIRDS):
+            wait_for(zr.at[:, 0:16], ZR + band)
         own = zs[pl.ds(pl.multiple_of(z * PAD, PAD), PAD), :]
         total = own + row_sum([zr[k] for k in range(2 * REACH)])
 
@@ -340,7 +356,7 @@
 
         for j in range(NCH):
             lanes = slice(j * LANES, (j + 1) * LANES)
-            block[:, lanes] = ef[pl.ds(j, NZ, stride=PAD), :].astype(jnp.bfloat16)
+            block[:, lanes] = ef[pl.ds(place(j), NZ, stride=PAD), :].astype(jnp.bfloat16)
 
         def features(x_of):
             return pl.ds(pl.multiple_of(first_chunk(x_of) * LANES, LANES), KW)
@@ -349,10 +365,16 @@
             to = lax.rem(x + k, NX)
             send(block.at[:, features(to)], part.at[x], KS, KR, at(to, z, pipe))
 
+        for q, lanes in SHARES.items():
+
+            @pl.when(pipe == q)
+            def _(lanes=lanes):
+                for k in range(1, NX):
+                    to = at(lax.rem(x + k, NX), z, 1)
+                    send(block.at[:, lanes], full.at[x, :, lanes], FS, FR, to)
+
         @pl.when(lead)
         def _():
-            for k in range(1, NX):
-                send(block, full.at[x], FS, FR, at(lax.rem(x + k, NX), z, pipe))
             full[x] = block[...]
 
         part[x] = block[:, features(x)]
@@ -417,8 +439,8 @@
 
     @pl.when(jnp.logical_not(worker))
     def _():
-        wait_for(wg.at[0:3], WAS)
-        wait_for(wz, WBS)
+        wait_for(hz, WAS)
+        wait_for(hz.at[0 : NZ - 1], WAS)
 
     @pl.when(worker)
     def _():
@@ -427,9 +449,11 @@
         wait_for(part.at[0:3], KS)
         wait_for(kp.at[0:3], PS)
 
-        @pl.when(lead)
-        def _():
-            wait_for(full.at[0:3], FS)
+        for q, lanes in SHARES.items():
+
+            @pl.when(pipe == q)
+            def _(lanes=lanes):
+                wait_for(full.at[0 : NX - 1, :, lanes], FS)
 
         @pl.when(jnp.logical_not(lead))
         def _():
@@ -496,7 +520,7 @@
     for j in range(NCH):
         lanes = slice(j * LANES, (j + 1) * LANES)
         for k in range(3):
-            rows_v[k, :, lanes] = step_v[k, j : j + 1, :]
+            rows_v[k, :, lanes] = step_v[k, place(j) : place(j) + 1, :]
     outs = [
         move(rows_v.at[k], out, 11 + k) for k, out in enumerate((master_out, one_out, two_out))
     ]
@@ -539,7 +563,7 @@
             pltpu.VMEM((WROWS, LANES), bf16),
             pltpu.VMEM((WPAD, LANES), bf16),
             pltpu.VMEM((WPAD, HEADS2), bf16),
-            pltpu.VMEM((4, WPAD, HEADS2), bf16),
+            pltpu.VMEM((NZ, WPAD, HEADS2), bf16),
             pltpu.VMEM((4, 4, WPAD, HEADS2), bf16),
             pltpu.VMEM((WPAD, LANES), f32),
             pltpu.VMEM((KW, HEADS2), bf16),
@@ -549,7 +573,7 @@
             pltpu.VMEM((1, HEAD_DIM), f32),
             pltpu.VMEM((3, PAD, LANES), f32),
             pltpu.VMEM((rows, kvw), bf16),
-            pltpu.SemaphoreType.DMA((39,)),
+            pltpu.SemaphoreType.DMA((SEMS,)),
         ],
         compiler_params=pltpu.CompilerParams(
             collective_id=0, has_side_effects=True, vmem_limit_bytes=VMEM_BYTES

time: 58.6 us -> 56.9 us (0.971)
  Pallas kernels: 57.8 us -> 56.2 us
    pallas_call x1, Pallas kernels: 53.9 us -> 52.3 us  [shards(): pl.pallas_call(comm_kernel, out_shape=(jax.ShapeDtypeStruct((NX, NZ, D),...]
where the time goes in v3:
time: 56.9 us; the launch traced here: 56.8 us
  Pallas kernels  56.2 us (99%)
  between operations  0.64 us (1%)
    pallas_call x1, Pallas kernels, shards(): pl.pallas_call(comm_kernel, out_shape=(jax.ShapeDtypeStruct((NX, NZ, D),...  52.3 us
    pallas_call x1, Pallas kernels, shards(): pl.pallas_call(look_up_kernel, out_shape=(line, line, line, jax.ShapeDtyp...  3.91 us

profile of v3, /device:TPU:1, one launch (start us, length us, event | category | flops | bytes accessed | tf_op | source)
XLA Modules:
  0.0 56.8 jit_solution(13086641870523319330)
XLA Ops:
  0.6 52.3 %sum_step_gather.1 = (bf16[4,16,5376]{2,1,0:T(8,128)(2,1)}, bf16[64,1024]{1,0:T(8,128)(2,1)}, f32[3,48,128]{2,1,0:T(8,128)}) custom-call(bf16[1,1,64,5376]{3,2,1,0:T(8,128)(2,1)} %grad.1, f32[1,5376]{1,0:T(1,128)} %master.1, f32[1,5376]{1,0:T(1,128)} %moment_one.1, f32[1,5376]{1,0:T(1,128)} %moment_two.1, bf16[84,128]{1,0:T(8,128)(2,1)} %weight.1, ...), custom_call_target="tpu_custom_call" | custom-call | tf_op jit(solution)/shard_map/sum_step_gather/pallas_call | solution.py:537
  52.9 3.9 %look_up.1 = (f32[1,5376]{1,0:T(1,128)}, f32[1,5376]{1,0:T(1,128)}, f32[1,5376]{1,0:T(1,128)}, bf16[256,5376]{1,0:T(8,128)(2,1)}, bf16[256,1024]{1,0:T(8,128)(2,1)}) custom-call(bf16[4,16,5376]{2,1,0:T(8,128)(2,1)} %get-tuple-element.13.table, bf16[64,1024]{1,0:T(8,128)(2,1)} %get-tuple-element.14.keys, f32[3,48,128]{2,1,0:T(8,128)} %get-tuple-element.15.step, ...), custom_call_target="tpu_custom_call" | custom-call | tf_op jit(solution)/shard_map/look_up/pallas_call | solution.py:587

commit v4 on v3

--- a/solution.py
+++ b/solution.py
@@ -18,7 +18,7 @@
 KW = KC * LANES
 HEADS2 = 2 * HEAD_DIM
 VMEM_BYTES = 60 * 2**20
-SHARES = {1: slice(0, 2688), 3: slice(2688, 4096), 6: slice(4096, D)}
+SHARES = {1: slice(0, 2688), 3: slice(2688, 4096), 7: slice(4096, D)}
 
 (
     XS, ZS, YS, YR0, YR1, W0S, W0R, WAS, WB,
@@ -48,11 +48,9 @@
     pipe = lax.axis_index("pipe")
     x, z = dp // NZ, lax.rem(dp, NZ)
     y = pipe // 2
-    far = y == NP // 2 - 1
-    worker = jnp.where(far, 2 * y, 2 * y + 1) == pipe
-    mate = jnp.where(lax.rem(pipe, 2) == 0, pipe + 1, pipe - 1)
-    source = jnp.logical_or(pipe == 0, pipe == NP - 1)
-    lead, last = pipe == 1, pipe == NP - 2
+    worker = lax.rem(pipe, 2) == 1
+    mate = jnp.where(worker, pipe - 1, pipe + 1)
+    lead, last = pipe == 1, pipe == NP - 1
     reducer = jnp.logical_or(lead, last)
 
     def at(x_to, z_to, pipe_to):
@@ -85,15 +83,15 @@
             tell(at(lax.rem(x + k, NX), z, pipe))
         tell((dp, mate))
 
-    @pl.when(reducer)
+    @pl.when(lead)
     def _():
         for k in range(1, NX):
-            tell(at(lax.rem(x + k, NX), z, mate))
+            tell(at(lax.rem(x + k, NX), z, 0))
 
     @pl.when(jnp.logical_not(worker))
     def _():
-        tell(at(x, away(1), pipe))
-        tell(at(x, away(-1), pipe))
+        for k in (1, -1, 2, -2):
+            tell(at(x, away(k), pipe))
 
     @pl.when(jnp.logical_or(pipe == 2, pipe == 4))
     def _():
@@ -105,13 +103,13 @@
 
     @pl.when(jnp.logical_not(last))
     def _():
-        tell((dp, NP - 2))
+        tell((dp, NP - 1))
 
     @pl.when(lead)
     def _():
         for k in range(NX):
-            for q in (3, 5, 6):
-                if k > 0 or q != 6:
+            for q in (3, 5, 7):
+                if k > 0 or q != 7:
                     tell(at(lax.rem(x + k, NX), z, q))
 
     def load(src, dst, which):
@@ -129,8 +127,8 @@
 
     peers = len(near) + NX - 1
     counts = {
-        0: 3 + NX - 1, NP - 1: 3 + NX - 1, 2: 3, 4: 3,
-        1: peers + NP - 1, 6: peers + NP - 1 + NX - 1, 3: peers + NX + 1, 5: peers + NX + 1,
+        0: 5 + NX - 1, 2: 5, 4: 5, 6: 5,
+        1: peers + NP - 1, 7: peers + NP - 1 + NX - 1, 3: peers + NX + 1, 5: peers + NX + 1,
     }
     for q, count in counts.items():
 
@@ -138,17 +136,20 @@
         def _(count=count):
             pl.semaphore_wait(barrier, count)
 
-    @pl.when(source)
-    def _():
-        for band in range(THIRDS):
-            lanes = slice(band * BAND * LANES, (band + 1) * BAND * LANES)
-            for k in (2, 1, 3, 0):
-                to = lax.rem(x + k, NX)
-                rows = pl.ds(pl.multiple_of(to * NZ, NZ), NZ)
-                send(
-                    grad.at[0, 0, rows, lanes], gx.at[x, :, lanes], XS, XR + band,
-                    at(to, z, mate),
-                )
+    for here in (0, NP - 1):
+
+        @pl.when(pipe == here)
+        def _(here=here):
+            for band in range(THIRDS):
+                lanes = slice(band * BAND * LANES, (band + 1) * BAND * LANES)
+                for k in (2, 1, 3, 0):
+                    to = lax.rem(x + k, NX)
+                    rows = pl.ds(pl.multiple_of(to * NZ, NZ), NZ)
+                    src, dst = grad.at[0, 0, rows, lanes], gx.at[x, :, lanes]
+                    if here and not k:
+                        load(src, dst, XR + band)
+                    else:
+                        send(src, dst, XS, XR + band, at(to, z, 1 if here == 0 else here))
 
     load_weight.wait()
     wc[...] = jnp.zeros_like(wc)
@@ -160,38 +161,39 @@
             wf[4 * q : 4 * q + WROWS, :] = wide
             wc[...] = wf[...].astype(jnp.bfloat16)
 
-    for high in (False, True):
-        lanes = slice(LANES, HEADS2) if high else slice(0, LANES)
-
-        @pl.when((lax.rem(pipe, 2) == 1) == high)
-        def _(lanes=lanes):
-            @pl.when(worker)
-            def _():
-                send(wc, wp.at[:, lanes], W0S, W0R, (dp, mate))
-
-            @pl.when(jnp.logical_not(worker))
-            def _():
-                wp[:, lanes] = wc[...]
-
-    def weights_round(step, away_step, count):
-        row = away(step)
-        if abs(step) < count:
-            send(hz.at[row], hz.at[row], WAS, WR + away_step, at(x, away(-1 if step > 0 else 1), pipe))
+    @pl.when(worker)
+    def _():
+        send(wc, wp.at[:, LANES:HEADS2], W0S, W0R, (dp, mate))
+
+    @pl.when(jnp.logical_not(worker))
+    def _():
+        wp[:, 0:LANES] = wc[...]
+
+    def weights_on(way, step):
+        row, first, limit = away(-way * step), (WR if way > 0 else WR + 8), (8 if way > 0 else 7)
+        if step % 2 == 0:
+            for k in (2, 1):
+                if step + k <= limit:
+                    to = at(x, away(way * k), pipe)
+                    send(hz.at[row], hz.at[row], WAS, first + step + k - 1, to)
+
+    def weights_in(way, step):
+        wait_for(wp, (WR if way > 0 else WR + 8) + step - 1)
+        weights_on(way, step)
+        row = away(-way * step)
         send(hz.at[row], wz.at[lax.rem(row, 4), row // 4], WAS, WB, (dp, mate))
 
     @pl.when(jnp.logical_not(worker))
     def _():
         wait_for(wc, W0R)
         hz[z] = wp[...]
-        send(hz.at[z], hz.at[z], WAS, WR, at(x, away(1), pipe))
-        send(hz.at[z], hz.at[z], WAS, WR + 8, at(x, away(-1), pipe))
+        weights_on(1, 0)
+        weights_on(-1, 0)
         send(hz.at[z], wz.at[lax.rem(z, 4), z // 4], WAS, WB, (dp, mate))
-        for step in range(1, 9):
-            wait_for(wp, WR + step - 1)
-            weights_round(-step, step, 8)
+        for step in (2, 1, 4, 3, 6, 5, 8, 7):
+            weights_in(1, step)
             if step < 8:
-                wait_for(wp, WR + 8 + step - 1)
-                weights_round(step, 8 + step, 7)
+                weights_in(-1, step)
 
     prior[...] = jnp.zeros_like(prior)
     for copy in load_state:
@@ -285,13 +287,13 @@
         @pl.when(lead)
         def _():
             yr[0] = total
-            for q in (3, 5, 6, 0, 2, 4, 7):
+            for q in (3, 5, 7, 0, 2, 4, 6):
                 send(yr.at[0], yr.at[0], YS, YR0, (dp, q))
 
         @pl.when(last)
         def _():
             yr[1] = total
-            for q in (1, 3, 5, 0, 2, 4, 7):
+            for q in (1, 3, 5, 0, 2, 4, 6):
                 send(yr.at[1], yr.at[1], YS, YR1, (dp, q))
 
     @pl.when(jnp.logical_not(lead))
@@ -427,9 +429,13 @@
 
     keep.wait()
 
-    @pl.when(source)
+    @pl.when(pipe == 0)
     def _():
         wait_for(gx, XS)
+
+    @pl.when(last)
+    def _():
+        wait_for(gx.at[0 : NX - 1], XS)
 
     @pl.when(reducer)
     def _():
@@ -482,18 +488,32 @@
 
     load_step = move(step, step_v, 6)
 
+    def finish(gives):
+        load_step.wait()
+        for j in range(NCH):
+            lanes = slice(j * LANES, (j + 1) * LANES)
+            for k in range(3):
+                rows_v[k, :, lanes] = step_v[k, place(j) : place(j) + 1, :]
+        for k, out in enumerate((master_out, one_out, two_out)):
+            gives.append(move(rows_v.at[k], out, 11 + k))
+        for copy in gives:
+            copy.wait()
+
     @pl.when(lead)
     def _():
         load_tokens = move(tokens, tokens_v, 7)
-        load_table = move(table, table_v, 8)
+        loads = []
+        for part in range(PARTS):
+            lanes = slice(part * width, (part + 1) * width)
+            loads.append(move(table.at[:, :, lanes], table_v.at[:, :, lanes], 14 + part))
         load_keys = move(keys, keys_v, 9)
         load_tokens.wait()
         rows = lax.broadcasted_iota(jnp.int32, (NX * NZ, tokens_v.shape[1]), 0)
         hot = jnp.where(rows == tokens_v[...], 1.0, 0.0).T.astype(jnp.bfloat16)
-        load_table.wait()
         gives = []
         for part in range(PARTS):
             lanes = slice(part * width, (part + 1) * width)
+            loads[part].wait()
             columns = table_v[:, :, lanes].reshape(NX * NZ, width)
             looked[:, lanes] = jnp.dot(
                 hot, columns, preferred_element_type=jnp.float32
@@ -504,8 +524,7 @@
             hot, keys_v[...], preferred_element_type=jnp.float32
         ).astype(jnp.bfloat16)
         gives.append(move(looked_keys, section_keys, 10))
-        for copy in gives:
-            copy.wait()
+        finish(gives)
 
     @pl.when(jnp.logical_not(lead))
     def _():
@@ -513,19 +532,7 @@
         looked_keys[...] = jnp.zeros_like(looked_keys)
         gives = [give(part) for part in range(PARTS)]
         gives.append(move(looked_keys, section_keys, 10))
-        for copy in gives:
-            copy.wait()
-
-    load_step.wait()
-    for j in range(NCH):
-        lanes = slice(j * LANES, (j + 1) * LANES)
-        for k in range(3):
-            rows_v[k, :, lanes] = step_v[k, place(j) : place(j) + 1, :]
-    outs = [
-        move(rows_v.at[k], out, 11 + k) for k, out in enumerate((master_out, one_out, two_out))
-    ]
-    for copy in outs:
-        copy.wait()
+        finish(gives)
 
 
 def shards(
@@ -601,7 +608,7 @@
             pltpu.VMEM((3, 1, D), f32),
             pltpu.VMEM((count, D), bf16),
             pltpu.VMEM((count, kvw), bf16),
-            pltpu.SemaphoreType.DMA((14,)),
+            pltpu.SemaphoreType.DMA((14 + PARTS,)),
         ],
         compiler_params=pltpu.CompilerParams(vmem_limit_bytes=VMEM_BYTES),
         name="look_up",

time: 56.9 us -> 53.4 us (0.938)
  Pallas kernels: 56.2 us -> 52.6 us
    pallas_call x1, Pallas kernels: 52.3 us -> 48.7 us  [shards(): pl.pallas_call(comm_kernel, out_shape=(jax.ShapeDtypeStruct((NX, NZ, D),...]
where the time goes in v4:
time: 53.4 us; the launch traced here: 53.2 us
  Pallas kernels  52.6 us (99%)
  between operations  0.64 us (1%)
    pallas_call x1, Pallas kernels, shards(): pl.pallas_call(comm_kernel, out_shape=(jax.ShapeDtypeStruct((NX, NZ, D),...  48.7 us
    pallas_call x1, Pallas kernels, shards(): pl.pallas_call(look_up_kernel, out_shape=(line, line, line, jax.ShapeDtyp...  3.84 us

profile of v4, /device:TPU:1, one launch (start us, length us, event | category | flops | bytes accessed | tf_op | source)
XLA Modules:
  0.0 53.2 jit_solution(14116760153696933010)
XLA Ops:
  0.6 48.7 %sum_step_gather.1 = (bf16[4,16,5376]{2,1,0:T(8,128)(2,1)}, bf16[64,1024]{1,0:T(8,128)(2,1)}, f32[3,48,128]{2,1,0:T(8,128)}) custom-call(bf16[1,1,64,5376]{3,2,1,0:T(8,128)(2,1)} %grad.1, f32[1,5376]{1,0:T(1,128)} %master.1, f32[1,5376]{1,0:T(1,128)} %moment_one.1, f32[1,5376]{1,0:T(1,128)} %moment_two.1, bf16[84,128]{1,0:T(8,128)(2,1)} %weight.1, ...), custom_call_target="tpu_custom_call" | custom-call | tf_op jit(solution)/shard_map/sum_step_gather/pallas_call | solution.py:544
  49.4 3.8 %look_up.1 = (f32[1,5376]{1,0:T(1,128)}, f32[1,5376]{1,0:T(1,128)}, f32[1,5376]{1,0:T(1,128)}, bf16[256,5376]{1,0:T(8,128)(2,1)}, bf16[256,1024]{1,0:T(8,128)(2,1)}) custom-call(bf16[4,16,5376]{2,1,0:T(8,128)(2,1)} %get-tuple-element.13.table, bf16[64,1024]{1,0:T(8,128)(2,1)} %get-tuple-element.14.keys, f32[3,48,128]{2,1,0:T(8,128)} %get-tuple-element.15.step, ...), custom_call_target="tpu_custom_call" | custom-call | tf_op jit(solution)/shard_map/look_up/pallas_call | solution.py:594

commit v5 on v4

--- a/solution.py
+++ b/solution.py
@@ -387,7 +387,7 @@
         )
         slot = y * NX + x
         kp[slot] = product.astype(jnp.bfloat16)
-        for k in range(NX):
+        for k in (2, 1, 3, 0):
             to = lax.rem(x + k, NX)
 
             def share(to=to):
@@ -466,7 +466,7 @@
             wait_for(kp.at[0], PS)
 
 
-PARTS = 6
+PARTS, TOKENS_AT_ONCE = 3, 64
 
 
 def look_up_kernel(
@@ -482,9 +482,9 @@
         copy.start()
         return copy
 
-    def give(part):
-        lanes = slice(part * width, (part + 1) * width)
-        return move(looked.at[:, lanes], section_input.at[:, lanes], part)
+    def give(first):
+        rows = slice(first, first + TOKENS_AT_ONCE)
+        return move(looked.at[rows], section_input.at[rows], first // TOKENS_AT_ONCE)
 
     load_step = move(step, step_v, 6)
 
@@ -511,14 +511,17 @@
         rows = lax.broadcasted_iota(jnp.int32, (NX * NZ, tokens_v.shape[1]), 0)
         hot = jnp.where(rows == tokens_v[...], 1.0, 0.0).T.astype(jnp.bfloat16)
         gives = []
-        for part in range(PARTS):
-            lanes = slice(part * width, (part + 1) * width)
-            loads[part].wait()
-            columns = table_v[:, :, lanes].reshape(NX * NZ, width)
-            looked[:, lanes] = jnp.dot(
-                hot, columns, preferred_element_type=jnp.float32
-            ).astype(jnp.bfloat16)
-            gives.append(give(part))
+        for copy in loads:
+            copy.wait()
+        for first in range(0, looked.shape[0], TOKENS_AT_ONCE):
+            tokens_now = slice(first, first + TOKENS_AT_ONCE)
+            for part in range(PARTS):
+                lanes = slice(part * width, (part + 1) * width)
+                looked[tokens_now, lanes] = jnp.dot(
+                    hot[tokens_now], table_v[:, :, lanes].reshape(NX * NZ, width),
+                    preferred_element_type=jnp.float32,
+                ).astype(jnp.bfloat16)
+            gives.append(give(first))
         load_keys.wait()
         looked_keys[...] = jnp.dot(
             hot, keys_v[...], preferred_element_type=jnp.float32
@@ -530,7 +533,7 @@
     def _():
         looked[...] = jnp.zeros_like(looked)
         looked_keys[...] = jnp.zeros_like(looked_keys)
-        gives = [give(part) for part in range(PARTS)]
+        gives = [give(first) for first in range(0, looked.shape[0], TOKENS_AT_ONCE)]
         gives.append(move(looked_keys, section_keys, 10))
         finish(gives)
 

time: 53.4 us -> 52.6 us (0.985)
  Pallas kernels: 52.6 us -> 51.8 us
where the time goes in v5:
time: 52.6 us; the launch traced here: 52.4 us
  Pallas kernels  51.8 us (98%)
  between operations  0.64 us (1%)
    pallas_call x1, Pallas kernels, shards(): pl.pallas_call(comm_kernel, out_shape=(jax.ShapeDtypeStruct((NX, NZ, D),...  48.4 us
    pallas_call x1, Pallas kernels, shards(): pl.pallas_call(look_up_kernel, out_shape=(line, line, line, jax.ShapeDtyp...  3.4 us

profile of v5, /device:TPU:1, one launch (start us, length us, event | category | flops | bytes accessed | tf_op | source)
XLA Modules:
  0.0 52.4 jit_solution(16545684654877129710)
XLA Ops:
  0.6 48.4 %sum_step_gather.1 = (bf16[4,16,5376]{2,1,0:T(8,128)(2,1)}, bf16[64,1024]{1,0:T(8,128)(2,1)}, f32[3,48,128]{2,1,0:T(8,128)}) custom-call(bf16[1,1,64,5376]{3,2,1,0:T(8,128)(2,1)} %grad.1, f32[1,5376]{1,0:T(1,128)} %master.1, f32[1,5376]{1,0:T(1,128)} %moment_one.1, f32[1,5376]{1,0:T(1,128)} %moment_two.1, bf16[84,128]{1,0:T(8,128)(2,1)} %weight.1, ...), custom_call_target="tpu_custom_call" | custom-call | tf_op jit(solution)/shard_map/sum_step_gather/pallas_call | solution.py:547
  49.0 3.4 %look_up.1 = (f32[1,5376]{1,0:T(1,128)}, f32[1,5376]{1,0:T(1,128)}, f32[1,5376]{1,0:T(1,128)}, bf16[256,5376]{1,0:T(8,128)(2,1)}, bf16[256,1024]{1,0:T(8,128)(2,1)}) custom-call(bf16[4,16,5376]{2,1,0:T(8,128)(2,1)} %get-tuple-element.13.table, bf16[64,1024]{1,0:T(8,128)(2,1)} %get-tuple-element.14.keys, f32[3,48,128]{2,1,0:T(8,128)} %get-tuple-element.15.step, ...), custom_call_target="tpu_custom_call" | custom-call | tf_op jit(solution)/shard_map/look_up/pallas_call | solution.py:597

commit v6 on v5

--- a/solution.py
+++ b/solution.py
@@ -354,7 +354,7 @@
         weights_join()
 
         wait_for(ezr.at[0 : NZ - 3], ER)
-        ef[...] = ezr[...].astype(jnp.float32).reshape(NZ * PAD, LANES)
+        ef[0 : NZ * PAD, :] = ezr[...].astype(jnp.float32).reshape(NZ * PAD, LANES)
 
         for j in range(NCH):
             lanes = slice(j * LANES, (j + 1) * LANES)
@@ -555,7 +555,7 @@
         out_specs=(hbm,) * 3,
         scratch_shapes=[
             pltpu.VMEM((NX, NZ, D), bf16),
-            pltpu.VMEM((NZ * PAD, LANES), f32),
+            pltpu.VMEM(((NZ + 1) * PAD, LANES), f32),
             pltpu.VMEM((NZ, PAD, LANES), bf16),
             pltpu.VMEM((2 * REACH, PAD, LANES), bf16),
             pltpu.VMEM((REACH, PAD, LANES), bf16),
@@ -566,7 +566,7 @@
             pltpu.VMEM((3, PAD, LANES), f32),
             pltpu.VMEM((PAD, LANES), bf16),
             pltpu.VMEM((NZ, PAD, LANES), bf16),
-            pltpu.VMEM((NZ * PAD, LANES), f32),
+            pltpu.VMEM(((NZ + 1) * PAD, LANES), f32),
             pltpu.VMEM((NZ, D), bf16),
             pltpu.VMEM((NX, NZ, D), bf16),
             pltpu.VMEM((NX, NZ, KW), bf16),

time: 52.6 us -> 52.6 us (level)
  no operation moved by 1% of the time
where the time goes in v6:
time: 52.6 us; the launch traced here: 52.4 us
  Pallas kernels  51.8 us (98%)
  between operations  0.64 us (1%)
    pallas_call x1, Pallas kernels, shards(): pl.pallas_call(comm_kernel, out_shape=(jax.ShapeDtypeStruct((NX, NZ, D),...  48.4 us
    pallas_call x1, Pallas kernels, shards(): pl.pallas_call(look_up_kernel, out_shape=(line, line, line, jax.ShapeDtyp...  3.4 us

profile of v6, /device:TPU:1, one launch (start us, length us, event | category | flops | bytes accessed | tf_op | source)
XLA Modules:
  0.0 52.4 jit_solution(5797400938987086348)
XLA Ops:
  0.6 48.4 %sum_step_gather.1 = (bf16[4,16,5376]{2,1,0:T(8,128)(2,1)}, bf16[64,1024]{1,0:T(8,128)(2,1)}, f32[3,48,128]{2,1,0:T(8,128)}) custom-call(bf16[1,1,64,5376]{3,2,1,0:T(8,128)(2,1)} %grad.1, f32[1,5376]{1,0:T(1,128)} %master.1, f32[1,5376]{1,0:T(1,128)} %moment_one.1, f32[1,5376]{1,0:T(1,128)} %moment_two.1, bf16[84,128]{1,0:T(8,128)(2,1)} %weight.1, ...), custom_call_target="tpu_custom_call" | custom-call | tf_op jit(solution)/shard_map/sum_step_gather/pallas_call | solution.py:547
  49.0 3.4 %look_up.1 = (f32[1,5376]{1,0:T(1,128)}, f32[1,5376]{1,0:T(1,128)}, f32[1,5376]{1,0:T(1,128)}, bf16[256,5376]{1,0:T(8,128)(2,1)}, bf16[256,1024]{1,0:T(8,128)(2,1)}) custom-call(bf16[4,16,5376]{2,1,0:T(8,128)(2,1)} %get-tuple-element.13.table, bf16[64,1024]{1,0:T(8,128)(2,1)} %get-tuple-element.14.keys, f32[3,48,128]{2,1,0:T(8,128)} %get-tuple-element.15.step, ...), custom_call_target="tpu_custom_call" | custom-call | tf_op jit(solution)/shard_map/look_up/pallas_call | solution.py:597
